TPU v7x, 32 devices: a whole 2x2x4 slice. The times are simulated.
32 devices in a mesh: dp: 8 (over y, x, core), fsdp: 4 (over z).
Axes of the slice: x: 2, y: 2, z: 4, core: 2. Of those that a mesh axis runs over, the one named last changes fastest.
Arguments:
- page_embed: bfloat16 [20480, 2048], P(('dp', 'fsdp')), may hold values from -6 to 6
- page_slot: int32 [20480], P(('dp', 'fsdp')), may hold values from 0 to 5119, as said below
- doc_ids: int32 [32, 640], P(('dp', 'fsdp')), may hold values from 0 to 9, never falling along the last dimension, each value on 1 to 128 neighbouring positions
- qkv_weight: bfloat16 [3, 2048, 1024], P(None, 'fsdp'), may hold values from -0.125 to 0.125
- out_weight: bfloat16 [1024, 2048], P(None, 'fsdp'), may hold values from -0.1875 to 0.1875
- fig_slot: int32 [512], P(('dp', 'fsdp')), may hold values from 0 to 639
- cap_slot: int32 [512], P(('dp', 'fsdp')), may hold values from 0 to 639
- logit_scale: float32 [1], replicated, may hold values from 10 to 30
- loss_cotangent: float32 [512], P(('dp', 'fsdp')), may hold values from 8 to 64
Outputs:
- page_grad: bfloat16 [20480, 2048], P(('dp', 'fsdp'))
- pair_loss: float32 [512], P(('dp', 'fsdp'))
Inputs may be any that keep to these rules, and one draw needn't show every extreme that they name: page_slot // 640 is the dp index of the owner and page_slot % 640 the slot there; within each group every slot is named by exactly one page; one device sends at most 100 pages to one owner, and every device sends exactly 100 to some owners. `doc_ids`: along a device's slots the document number never falls; each of the 10 documents has 1 to 128 slots, one exactly 128. `fig_slot`: a slot of the pair's own device. `cap_slot`: a slot of the pair's own device.
All inputs are finite; a program needn't handle non-finite values.
Results may differ from a plain program's by a relative error of at most 0.017.
Values may be sent and summed in bfloat16 or wider, within the bound.
A program may use at most 192 MiB of HBM per device.

v0:
```python
import math

import jax
import jax.numpy as jnp
from jax import lax
from jax.sharding import PartitionSpec as P

HD = 64
EPSILON = 1e-06
FIXED = 2.0**20
BF = jnp.bfloat16
F32 = jnp.float32


def mm(a, b):
    return jnp.dot(a, b, preferred_element_type=F32)


def mmt(a, b):
    return lax.dot_general(a, b, (((1,), (1,)), ((), ())), preferred_element_type=F32)


def tmm(a, b):
    return lax.dot_general(a, b, (((0,), (0,)), ((), ())), preferred_element_type=F32)


def split3(x):
    hi = x.astype(BF)
    rest = x - hi.astype(F32)
    mid = rest.astype(BF)
    low = (rest - mid.astype(F32)).astype(BF)
    return jnp.concatenate([hi, mid, low], axis=0)


def exact_mm(x, emb):
    count = x.shape[0]
    parts = mm(split3(x), emb)
    return parts[:count] + parts[count : 2 * count] + parts[2 * count :]


def expand(x, head_mask):
    return (x[None] * head_mask.astype(x.dtype)).reshape(-1, x.shape[1])


def collapse(x, head_mask, rows):
    return jnp.sum(x.reshape(-1, rows, x.shape[1]) * head_mask, axis=0)


def body(
    page_embed,
    page_slot,
    doc_ids,
    qkv_weight,
    out_weight,
    fig_slot,
    cap_slot,
    logit_scale,
    loss_cotangent,
):
    dp_count = lax.axis_size("dp")
    me = lax.axis_index("dp")
    half = me % 2
    row_count, width = page_embed.shape
    capacity = -(-(5 * row_count) // (4 * dp_count))
    capacity = -(-capacity // 8) * 8
    total = dp_count * capacity
    pair_count = fig_slot.shape[0]
    hdim = qkv_weight.shape[2]
    half_width = hdim // 2
    pair_swap = [(i, i ^ 1) for i in range(dp_count)]

    def gather_half(index):
        piece = lax.dynamic_slice_in_dim(qkv_weight[index], half * half_width, half_width, 1)
        return lax.all_gather(piece, "fsdp", axis=0, tiled=True)

    key_m, query_m, value_m = gather_half(1), gather_half(0), gather_half(2)
    key_o, query_o, value_o = [lax.ppermute(w, "dp", pair_swap) for w in (key_m, query_m, value_m)]
    out_rows = hdim // dp_count
    out_piece = lax.dynamic_slice_in_dim(out_weight, me * out_rows, out_rows, 0)
    out_piece = lax.all_gather(out_piece, "fsdp", axis=1, tiled=True)
    out_full = lax.all_gather(out_piece, "dp", axis=0, tiled=True)

    owner_idx = page_slot // row_count
    slot_idx = page_slot % row_count
    onehot = (owner_idx[:, None] == jnp.arange(dp_count)[None, :]).astype(jnp.int32)
    rank_idx = jnp.sum((jnp.cumsum(onehot, axis=0) - onehot) * onehot, axis=1)
    place_idx = owner_idx * capacity + rank_idx
    place = jnp.arange(total)[:, None] == place_idx[None, :]
    send_ids = jnp.sum(jnp.where(place, slot_idx[None, :] + 1, 0), axis=1) - 1
    fixed_ct = (loss_cotangent * FIXED).astype(jnp.int32)
    send_ints = jnp.concatenate(
        [
            send_ids.reshape(dp_count, capacity),
            jnp.broadcast_to(fixed_ct[None, :], (dp_count, pair_count)),
        ],
        axis=1,
    )
    recv_ints = lax.all_to_all(send_ints, "dp", split_axis=0, concat_axis=0, tiled=True)
    send_rows = mm(place.astype(BF), page_embed).astype(BF)
    rows = lax.all_to_all(send_rows, "dp", split_axis=0, concat_axis=0, tiled=True)

    ids = recv_ints[:, :capacity].reshape(-1)
    group_ct = recv_ints[:, capacity:].reshape(-1).astype(F32) * (1.0 / FIXED)
    doc_row = doc_ids[0]
    slot_range = jnp.arange(row_count)
    row_docs = (
        jnp.sum(jnp.where(ids[:, None] == slot_range[None, :], doc_row[None, :] + 1, 0), axis=1) - 1
    )
    slots = jnp.concatenate([fig_slot, cap_slot])
    slot_docs = jnp.sum(jnp.where(slots[:, None] == slot_range[None, :], doc_row[None, :], 0), axis=1)
    picked = (slots[:, None] == ids[None, :]).astype(BF)
    same_doc = slot_docs[:, None] == row_docs[None, :]
    pick_count = slots.shape[0]

    picked_rows = mm(picked, rows).astype(BF)
    scale = 1.0 / math.sqrt(HD)
    heads = half_width // HD
    head_mask = (
        jnp.arange(half_width)[None, None, :] // HD == jnp.arange(heads)[:, None, None]
    ).astype(F32)

    state = []
    mixes = []
    for w_q, w_k, w_v in ((query_m, key_m, value_m), (query_o, key_o, value_o)):
        key = mm(rows, w_k).astype(BF)
        query = expand(mm(picked_rows, w_q).astype(BF), head_mask)
        value = mm(rows, w_v).astype(BF)
        scores = mmt(query, key).reshape(heads, pick_count, total) * scale
        weights = jnp.where(same_doc[None], jnp.exp(jnp.where(same_doc[None], scores, -1e30)), 0.0)
        prob = weights / jnp.sum(weights, axis=2, keepdims=True)
        prob_b = prob.astype(BF).reshape(heads * pick_count, total)
        mixes.append(collapse(mm(prob_b, value), head_mask, pick_count).astype(BF))
        state.append((query, key, value, prob, prob_b))
    first = jnp.where(half == 0, mixes[0], mixes[1])
    second = jnp.where(half == 0, mixes[1], mixes[0])
    attn_out = mm(jnp.concatenate([first, second], axis=1), out_full)

    vec = picked_rows.astype(F32) + attn_out
    inv = lax.rsqrt(jnp.sum(vec * vec, axis=1, keepdims=True) + EPSILON)
    unit = vec * inv
    all_emb = lax.all_gather(unit.astype(BF), "dp", axis=0)
    all_fig = all_emb[:, :pair_count].reshape(-1, width)
    all_cap = all_emb[:, pair_count:].reshape(-1, width)
    logit_mult = logit_scale[0]
    logits = logit_mult * mmt(all_fig, all_cap)
    row_lse = jnp.log(jnp.sum(jnp.exp(logits), axis=1))
    col_lse = jnp.log(jnp.sum(jnp.exp(logits), axis=0))
    group_pairs = logits.shape[0]
    eye = jnp.arange(group_pairs)[:, None] == jnp.arange(group_pairs)[None, :]
    diag = jnp.sum(jnp.where(eye, logits, 0.0), axis=1)
    eye = eye.astype(F32)
    all_loss = 0.5 * (row_lse - diag) + 0.5 * (col_lse - diag)
    pair_loss = lax.dynamic_slice_in_dim(all_loss, me * pair_count, pair_count, 0)
    coef = 0.5 * group_ct[:, None] * (jnp.exp(logits - row_lse[:, None]) - eye) + 0.5 * (
        jnp.exp(logits - col_lse[None, :]) - eye
    ) * group_ct[None, :]
    coef_f = lax.dynamic_slice_in_dim(coef, me * pair_count, pair_count, 0)
    coef_c = lax.dynamic_slice_in_dim(coef.T, me * pair_count, pair_count, 0)
    grad = logit_mult * jnp.concatenate(
        [exact_mm(coef_f, all_cap), exact_mm(coef_c, all_fig)], axis=0
    )
    dvec = inv * (grad - unit * jnp.sum(unit * grad, axis=1, keepdims=True))

    dmix = mmt(dvec.astype(BF), out_full).astype(BF)
    low, high = dmix[:, :half_width], dmix[:, half_width:]
    dmix_m = jnp.where(half == 0, low, high)
    dmix_o = jnp.where(half == 0, high, low)
    row_ct = 0.0
    picked_ct = dvec
    for (query, key, value, prob, prob_b), w_q, w_k, w_v, dmix_h in (
        (state[0], query_m, key_m, value_m, dmix_m),
        (state[1], query_o, key_o, value_o, dmix_o),
    ):
        dmix_e = expand(dmix_h, head_mask)
        dprob = mmt(dmix_e, value).reshape(heads, pick_count, total)
        dscore = prob * (dprob - jnp.sum(dprob * prob, axis=2, keepdims=True)) * scale
        dscore = dscore.astype(BF).reshape(heads * pick_count, total)
        dquery = collapse(mm(dscore, key), head_mask, pick_count).astype(BF)
        dkey = tmm(dscore, query).astype(BF)
        dvalue = tmm(prob_b, dmix_e).astype(BF)
        row_ct = row_ct + mmt(dkey, w_k) + mmt(dvalue, w_v)
        picked_ct = picked_ct + mmt(dquery, w_q)
    ct_hi = picked_ct.astype(BF)
    ct_lo = (picked_ct - ct_hi.astype(F32)).astype(BF)
    row_ct = row_ct + tmm(
        jnp.concatenate([picked, picked], axis=0), jnp.concatenate([ct_hi, ct_lo], axis=0)
    )
    home = lax.all_to_all(row_ct.astype(BF), "dp", split_axis=0, concat_axis=0, tiled=True)
    page_grad = tmm(place.astype(BF), home).astype(BF)
    return (page_grad, pair_loss)


def solution(mesh):
    return jax.shard_map(
        body,
        mesh=mesh,
        in_specs=(
            P(("dp", "fsdp"), None),
            P(("dp", "fsdp")),
            P(("dp", "fsdp"), None),
            P(None, "fsdp", None),
            P(None, "fsdp"),
            P(("dp", "fsdp")),
            P(("dp", "fsdp")),
            P(),
            P(("dp", "fsdp")),
        ),
        out_specs=(P(("dp", "fsdp"), None), P(("dp", "fsdp"))),
        check_vma=False,
    )
```

profile of v0, /device:TPU:0, one launch (start us, length us, event | category | flops | bytes accessed | tf_op | source)
XLA Modules:
  0.0 354.1 jit_solution(12833776451179200569)
XLA Ops:
  7.2 3.7 %fusion.148 = (bf16[1,512,1024]{2,1,0:T(8,128)(2,1)}, bf16[1,512,1024]{2,1,0:T(8,128)(2,1)}, bf16[1,512,1024]{2,1,0:T(8,128)(2,1)}) fusion(bf16[3,512,1024]{2,1,0:T(8,128)(2,1)} %param.12), kind=kLoop, calls=%fused_computation.217 | loop fusion | bytes 6291456 | tf_op jit(solution)/shard_map/slice | solution.py:73
  11.0 1.9 constant_dynamic-slice_fusion.3
  13.0 1.9 constant_dynamic-slice_fusion.2
  14.9 1.9 constant_dynamic-slice_fusion.1
  17.0 1.4 reduce-window.6
  19.0 0.3 select_reduce_fusion.1
  19.4 0.6 pad_add_fusion
  20.0 5.2 %all-to-all-start = ((s32[8,1,120]{2,1,0:T(1,128)}), s32[8,1,120]{2,1,0:T(1,128)S(1)}, u32[]{:S(2)}, u32[]{:S(2)}) async-start(s32[8,1,120]{2,1,0:T(1,128)} %bitcast.4), calls=%async_computation | async-start | bytes 8192 | tf_op jit(solution)/shard_map/all_to_all | solution.py:98
  25.2 0.9 constant_dynamic-slice_fusion
  26.1 23.3 %all_gather.24 = bf16[128,2048]{1,0:T(8,128)(2,1)} all-gather(bf16[128,512]{1,0:T(8,128)(2,1)S(1)} %constant_dynamic-slice_fusion), channel_id=1, replica_groups=mesh['dp'=8,'fsdp'=4] {'fsdp'}, dimensions={1}, use_global_device_ids=true | all-gather | bytes 655360 | tf_op jit(solution)/shard_map/all_gather | solution.py:80
  49.4 4.2 %convolution_convert_fusion = bf16[832,2048]{1,0:T(8,128)(2,1)} fusion(bf16[640,2048]{1,0:T(8,128)(2,1)S(1)} %copy-done, s32[640]{0:T(1024)S(1)} %get-tuple-element.25), kind=kOutput, calls=%fused_computation.3 | convolution fusion | flops 2183274496 | bytes 6031872 | tf_op jit(solution)/shard_map/dot_general | solution.py:16
  53.7 4.6 %all-to-all-start.1 = ((bf16[8,104,2048]{2,1,0:T(8,128)(2,1)}), bf16[8,104,2048]{2,1,0:T(8,128)(2,1)}, u32[]{:S(2)}, u32[]{:S(2)}) async-start(bf16[8,104,2048]{2,1,0:T(8,128)(2,1)} %bitcast.112), calls=%async_computation.1 | async-start | bytes 6815744 | tf_op jit(solution)/shard_map/all_to_all | solution.py:100
  58.3 0.2 all-gather.18.cloned.1.call-start
  58.7 0.2 select_reduce_fusion.2
  59.0 0.4 select_reduce_fusion
  59.5 10.5 %all-gather.12.cloned.1.call-done = bf16[1,2048,512]{2,1,0:T(8,128)(2,1)} async-done(((bf16[1,512,512]{2,1,0:T(8,128)(2,1)}), bf16[1,2048,512]{2,1,0:T(8,128)(2,1)}) %all-gather.12.cloned.1.call-update) | async-done | bytes 2097168 | tf_op jit(solution)/shard_map/all_gather | solution.py:74
  70.0 29.0 %all-to-all-done.1 = bf16[8,104,2048]{2,1,0:T(8,128)(2,1)} async-done(((bf16[8,104,2048]{2,1,0:T(8,128)(2,1)}), bf16[8,104,2048]{2,1,0:T(8,128)(2,1)}, u32[]{:S(2)}, u32[]{:S(2)}) %all-to-all-start.1) | async-done | bytes 3407904 | tf_op jit(solution)/shard_map/all_to_all | solution.py:100
  99.0 2.7 convolution_convert_fusion.2
  101.7 14.6 %all-gather.14.cloned.1.call-done = bf16[1,2048,512]{2,1,0:T(8,128)(2,1)} async-done(((bf16[1,512,512]{2,1,0:T(8,128)(2,1)}), bf16[1,2048,512]{2,1,0:T(8,128)(2,1)}) %all-gather.14.cloned.1.call-update) | async-done | bytes 2097168 | tf_op jit(solution)/shard_map/all_gather | solution.py:74
  116.3 46.3 %all-gather.16.cloned.1.call-done = bf16[1,2048,512]{2,1,0:T(8,128)(2,1)} async-done(((bf16[1,512,512]{2,1,0:T(8,128)(2,1)}), bf16[1,2048,512]{2,1,0:T(8,128)(2,1)}) %all-gather.16.cloned.1.call-update) | async-done | bytes 2097168 | tf_op jit(solution)/shard_map/all_gather | solution.py:74
  162.6 0.4 convolution_convert_fusion.9
  163.0 1.1 copy-done.36
  164.1 4.9 %fusion.14 = bf16[832,512,1]{1,0,2:T(8,128)(2,1)} fusion(bf16[832,2048]{1,0:T(8,128)(2,1)} %bitcast.7, bf16[1,2048,512]{2,1,0:T(8,128)(2,1)S(1)} %copy-done.36), kind=kOutput, calls=%fused_computation.35 | convolution fusion | flops 1745256448 | bytes 6356992 | tf_op jit(solution)/shard_map/dot_general | solution.py:16
  169.1 1.8 fusion.41
  170.9 4.9 %fusion.15 = bf16[832,512,1]{1,0,2:T(8,128)(2,1)S(1)} fusion(bf16[832,2048]{1,0:T(8,128)(2,1)} %bitcast.7, bf16[1,2048,512]{2,1,0:T(8,128)(2,1)} %all-gather.16.cloned.1.call-done), kind=kOutput, calls=%fused_computation.36 | convolution fusion | flops 1745256448 | bytes 6356992 | tf_op jit(solution)/shard_map/dot_general | solution.py:16
  175.8 0.4 fusion.20
  176.3 2.0 convolution_convert_fusion.8
  178.3 5.5 %fusion.16 = bf16[832,512,1]{1,0,2:T(8,128)(2,1)} fusion(bf16[832,2048]{1,0:T(8,128)(2,1)} %bitcast.7, bf16[2048,512]{1,0:T(8,128)(2,1)} %collective-permute-done.1), kind=kOutput, calls=%fused_computation.37 | convolution fusion | flops 1745256448 | bytes 6356992 | tf_op jit(solution)/shard_map/dot_general | solution.py:16
  183.8 1.9 fusion.39
  185.8 4.9 %fusion.17 = bf16[832,512,1]{1,0,2:T(8,128)(2,1)S(1)} fusion(bf16[832,2048]{1,0:T(8,128)(2,1)} %bitcast.7, bf16[2048,512]{1,0:T(8,128)(2,1)} %collective-permute-done.2), kind=kOutput, calls=%fused_computation.38 | convolution fusion | flops 1745256448 | bytes 6356992 | tf_op jit(solution)/shard_map/dot_general | solution.py:16
  190.7 0.4 fusion.21
  191.1 0.4 copy-done.7
  191.6 8.2 %all-gather.10.cloned.1.call-done = bf16[1024,2048]{1,0:T(8,128)(2,1)} async-done(((bf16[128,2048]{1,0:T(8,128)(2,1)}), bf16[1024,2048]{1,0:T(8,128)(2,1)}) %all-gather.10.cloned.1.call-update) | async-done | bytes 4194320 | tf_op jit(solution)/shard_map/all_gather | solution.py:81
  199.8 3.1 multiply_reduce_fusion.3
  202.9 0.7 multiply_convert_fusion
  204.5 0.7 broadcast_compare_fusion
  205.2 22.1 %all-gather.18.cloned.1.call-done = bf16[256,2048]{1,0:T(8,128)(2,1)} async-done(((bf16[32,2048]{1,0:T(8,128)(2,1)}), bf16[256,2048]{1,0:T(8,128)(2,1)}) %all-gather.18.cloned.1.call-update) | async-done | bytes 1048592 | tf_op jit(solution)/shard_map/all_gather | solution.py:141
  227.3 1.3 fusion.149
  228.6 0.8 copy-done.3
  229.4 0.4 select_reduce_fusion.3
  229.8 0.5 add_multiply_fusion
  230.8 1.3 fusion.105
  232.1 0.2 fusion.111
  232.4 0.2 multiply_reduce_fusion.2
  232.6 3.7 %convolution_convert_fusion.7 = bf16[32,1024]{1,0:T(8,128)(2,1)S(1)} fusion(bf16[1024,2048]{1,0:T(8,128)(2,1)} %all-gather.10.cloned.1.call-done, f32[32,2048]{1,0:T(8,128)S(1)} %get-tuple-element.34, f32[16,2048]{1,0:T(8,128)S(1)} %get-tuple-element.36, f32[16,2048]{1,0:T(8,128)S(1)} %get-tuple-element.37, f32[32]{0:T(128)S(1)} %multiply_reduce_fusion.2, ...), kind=kOutput, calls=%fused_computation.49 | convolution fusion | flops 134709248 | bytes 4784388 | tf_op jit(solution)/shard_map/dot_general | solution.py:20
  236.3 0.6 broadcast_select_fusion
  236.9 0.6 copy-done.11
  237.5 1.5 fusion.48
  239.0 2.9 fusion.23
  241.9 3.0 bitcast_convert_fusion.1
  244.8 2.9 fusion.52
  247.7 3.5 fusion.22
  251.2 3.6 %bitcast_convert_fusion.3 = bf16[832,512]{1,0:T(8,128)(2,1)} fusion(f32[8,32,832]{2,1,0:T(8,128)} %copy-done.9, f32[8,32,832]{2,1,0:T(8,128)} %fusion.52, bf16[8,512]{1,0:T(8,128)(2,1)} %copy-done.14, bf16[32,512]{1,0:T(8,128)(2,1)} %copy-done.22), kind=kOutput, calls=%fused_computation.16 | convolution fusion | flops 219726912 | bytes 2596864 | tf_op jit(solution)/shard_map/dot_general | solution.py:24
  254.8 1.5 convolution_add_fusion.1
  256.3 2.3 subtract_convert_fusion
  258.6 3.9 %fusion.58 = f32[832,2048]{1,0:T(8,128)} fusion(bf16[32,2048]{1,0:T(8,128)(2,1)S(1)} %get-tuple-element.7, bf16[32,2048]{1,0:T(8,128)(2,1)S(1)} %get-tuple-element.8, pred[32,832]{1,0:T(32,128)(4,1)S(1)} %copy-done.17), kind=kOutput, calls=%fused_computation.80 | convolution fusion | flops 218681344 | bytes 7104512 | tf_op jit(solution)/shard_map/dot_general | solution.py:24
  262.6 6.7 %fusion.36 = f32[832,2048]{1,0:T(8,128)} fusion(f32[8,32,832]{2,1,0:T(8,128)S(1)} %copy-done.10, bf16[32,512]{1,0:T(8,128)(2,1)S(1)} %copy-done.13, bf16[8,512]{1,0:T(8,128)(2,1)S(1)} %copy-done.16, bf16[1,2048,512]{2,1,0:T(8,128)(2,1)} %all-gather.16.cloned.1.call-done), kind=kOutput, calls=%fused_computation.59 | convolution fusion | flops 1963704320 | bytes 9805824 | tf_op jit(solution)/shard_map/dot_general | solution.py:20
  269.3 6.4 %fusion.135 = f32[832,2048]{1,0:T(8,128)} fusion(bf16[832,512]{1,0:T(8,128)(2,1)S(1)} %copy-done.41, bf16[1,2048,512]{2,1,0:T(8,128)(2,1)} %all-gather.14.cloned.1.call-done), kind=kOutput, calls=%fused_computation.206 | convolution fusion | flops 1744830464 | bytes 9764864 | tf_op jit(solution)/shard_map/dot_general | solution.py:20
  275.7 6.4 %fusion.154 = f32[832,2048]{1,0:T(8,128)} fusion(bf16[832,512]{1,0:T(8,128)(2,1)S(1)} %copy-done.40, bf16[2048,512]{1,0:T(8,128)(2,1)} %collective-permute-done.1), kind=kOutput, calls=%fused_computation.219 | convolution fusion | flops 1744830464 | bytes 9764864 | tf_op jit(solution)/shard_map/dot_general | solution.py:20
  282.0 13.7 %add_convert_fusion = bf16[832,2048]{1,0:T(8,128)(2,1)} fusion(f32[832,2048]{1,0:T(8,128)} %fusion.58, f32[832,2048]{1,0:T(8,128)} %fusion.154, f32[832,2048]{1,0:T(8,128)} %fusion.135, f32[832,2048]{1,0:T(8,128)} %fusion.36, bf16[2048,512]{1,0:T(8,128)(2,1)} %collective-permute-done.2, f32[8,32,832]{2,1,0:T(8,128)S(1)} %copy-done.5, ...), kind=kOutput, calls=%fused_computation.2 | convolution fusion | flops 1972224000 | bytes 33660928 | tf_op jit(solution)/shard_map/dot_general | solution.py:20
  295.8 4.9 %all-to-all-start.2 = ((bf16[8,104,2048]{2,1,0:T(8,128)(2,1)}), bf16[8,104,2048]{2,1,0:T(8,128)(2,1)}, u32[]{:S(2)}, u32[]{:S(2)}) async-start(bf16[8,104,2048]{2,1,0:T(8,128)(2,1)} %bitcast.106), calls=%async_computation.2 | async-start | bytes 6815744 | tf_op jit(solution)/shard_map/all_to_all | solution.py:188
  300.6 0.6 dynamic_slice.36
  301.2 39.8 %all-to-all-done.2 = bf16[8,104,2048]{2,1,0:T(8,128)(2,1)} async-done(((bf16[8,104,2048]{2,1,0:T(8,128)(2,1)}), bf16[8,104,2048]{2,1,0:T(8,128)(2,1)}, u32[]{:S(2)}, u32[]{:S(2)}) %all-to-all-start.2) | async-done | bytes 3407904 | tf_op jit(solution)/shard_map/all_to_all | solution.py:188
  341.1 6.5 %convolution_convert_fusion.1 = bf16[640,2048]{1,0:T(8,128)(2,1)} fusion(bf16[832,2048]{1,0:T(8,128)(2,1)} %bitcast.25, s32[640]{0:T(1024)S(1)} %copy-done.27), kind=kOutput, calls=%fused_computation.4 | convolution fusion | flops 2182881280 | bytes 6031872 | tf_op jit(solution)/shard_map/dot_general | solution.py:24
  (126 shorter events, 2.1 us)
Async XLA Ops:
  7.2 42.3 %copy-start = (bf16[640,2048]{1,0:T(8,128)(2,1)S(1)}, bf16[640,2048]{1,0:T(8,128)(2,1)}, u32[]{:S(2)}) copy-start(bf16[640,2048]{1,0:T(8,128)(2,1)} %param.9) | copy-start | bytes 7864324
  7.2 62.9 %all-gather.12.cloned.1.call-start = ((), (), s32[]{:S(2)}) async-start(), calls=%async_computation.4 | async-start | bytes 2621440 | tf_op jit(solution)/shard_map/all_gather | solution.py:74
  11.0 5.8 %copy-start.37 = (f32[16]{0:T(128)S(1)}, f32[16]{0:T(128)}, u32[]{:S(2)}) copy-start(f32[16]{0:T(128)} %param.17) | copy-start | bytes 196
  11.0 5.9 %copy-start.25 = (s32[640]{0:T(1024)S(1)}, s32[640]{0:T(1024)}, u32[]{:S(2)}) copy-start(s32[640]{0:T(1024)} %param.10) | copy-start | bytes 7684
  12.9 103.4 %all-gather.14.cloned.1.call-start = ((), (), s32[]{:S(2)}) async-start(), calls=%async_computation.5 | async-start | bytes 2621440 | tf_op jit(solution)/shard_map/all_gather | solution.py:74
  14.9 147.7 %all-gather.16.cloned.1.call-start = ((), (), s32[]{:S(2)}) async-start(), calls=%async_computation.6 | async-start | bytes 2621440 | tf_op jit(solution)/shard_map/all_gather | solution.py:74
  19.0 34.7 %copy-start.26 = (s32[640]{0:T(1024)}, s32[640]{0:T(1024)S(1)}, u32[]{:S(2)}) copy-start(s32[640]{0:T(1024)S(1)} %get-tuple-element.25) | copy-start | bytes 7684
  20.0 33.7 %all-to-all-start = ((s32[8,1,120]{2,1,0:T(1,128)}), s32[8,1,120]{2,1,0:T(1,128)S(1)}, u32[]{:S(2)}, u32[]{:S(2)}) async-start(s32[8,1,120]{2,1,0:T(1,128)} %bitcast.4), calls=%async_computation | async-start | bytes 8192 | tf_op jit(solution)/shard_map/all_to_all | solution.py:98
  25.1 174.6 %all-gather.10.cloned.1.call-start = ((), (), s32[]{:S(2)}) async-start(), calls=%async_computation.3 | async-start | bytes 4718592 | tf_op jit(solution)/shard_map/all_gather | solution.py:81
  53.7 5.2 %copy-start.20 = (s32[8,1,120]{2,1,0:T(1,128)}, s32[8,1,120]{2,1,0:T(1,128)S(1)}, u32[]{:S(2)}) copy-start(s32[8,1,120]{2,1,0:T(1,128)S(1)} %all-to-all-done) | copy-start | bytes 11524
  53.7 4.9 %copy-start.38 = (s32[16]{0:T(128)S(1)}, s32[16]{0:T(128)}, u32[]{:S(2)}) copy-start(s32[16]{0:T(128)} %param.15) | copy-start | bytes 196
  53.7 4.9 %copy-start.39 = (s32[16]{0:T(128)S(1)}, s32[16]{0:T(128)}, u32[]{:S(2)}) copy-start(s32[16]{0:T(128)} %param.14) | copy-start | bytes 196
  53.7 5.0 %copy-start.34 = (s32[1,640]{1,0:T(1,128)S(1)}, s32[1,640]{1,0:T(1,128)}, u32[]{:S(2)}) copy-start(s32[1,640]{1,0:T(1,128)} %param.11) | copy-start | bytes 7684
  53.7 45.3 %all-to-all-start.1 = ((bf16[8,104,2048]{2,1,0:T(8,128)(2,1)}), bf16[8,104,2048]{2,1,0:T(8,128)(2,1)}, u32[]{:S(2)}, u32[]{:S(2)}) async-start(bf16[8,104,2048]{2,1,0:T(8,128)(2,1)} %bitcast.112), calls=%async_computation.1 | async-start | bytes 6815744 | tf_op jit(solution)/shard_map/all_to_all | solution.py:100
  58.3 169.0 %all-gather.18.cloned.1.call-start = ((), (), s32[]{:S(2)}) async-start(), calls=%async_computation.7 | async-start | bytes 1179648 | tf_op jit(solution)/shard_map/all_gather | solution.py:141
  58.7 104.3 %copy-start.32 = (s32[32]{0:T(128)}, s32[32]{0:T(128)S(1)}, u32[]{:S(2)}) copy-start(s32[32]{0:T(128)S(1)} %pad_add_fusion.1) | copy-start | bytes 388
  58.9 124.9 %copy-start.14 = (bf16[8,512]{1,0:T(8,128)(2,1)}, bf16[8,512]{1,0:T(8,128)(2,1)S(1)}, u32[]{:S(2)}) copy-start(bf16[8,512]{1,0:T(8,128)(2,1)S(1)} %get-tuple-element.29) | copy-start | bytes 24580
  59.0 104.0 %copy-start.18 = (s32[832]{0:T(1024)}, s32[832]{0:T(1024)S(1)}, u32[]{:S(2)}) copy-start(s32[832]{0:T(1024)S(1)} %eq.206) | copy-start | bytes 9988
  70.0 92.5 %copy-start.2 = (bf16[1,2048,512]{2,1,0:T(8,128)(2,1)S(1)}, bf16[1,2048,512]{2,1,0:T(8,128)(2,1)}, u32[]{:S(2)}) copy-start(bf16[1,2048,512]{2,1,0:T(8,128)(2,1)} %all-gather.12.cloned.1.call-done) | copy-start | bytes 6291460
  70.0 106.2 %collective-permute-start = (bf16[2048,512]{1,0:T(8,128)(2,1)}, bf16[2048,512]{1,0:T(8,128)(2,1)}, u32[]{:S(2)}, u32[]{:S(2)}) collective-permute-start(bf16[2048,512]{1,0:T(8,128)(2,1)} %bitcast.107), channel_id=1, source_target_pairs={{0,4},{4,0},{8,12},{12,8},{16,20},{20,16},{24,28},{28,24},{1,5},{5... | collective-permute-start | bytes 6291464 | tf_op jit(solution)/shard_map/ppermute | solution.py:77
  116.3 62.0 %collective-permute-start.1 = (bf16[2048,512]{1,0:T(8,128)(2,1)}, bf16[2048,512]{1,0:T(8,128)(2,1)}, u32[]{:S(2)}, u32[]{:S(2)}) collective-permute-start(bf16[2048,512]{1,0:T(8,128)(2,1)} %bitcast.118), channel_id=1, source_target_pairs={{0,4},{4,0},{8,12},{12,8},{16,20},{20,16},{24,28},{28,24},{1,5},{5... | collective-permute-start | bytes 6291464 | tf_op jit(solution)/shard_map/ppermute | solution.py:77
  162.5 1.6 copy-start.36
  162.5 23.2 %collective-permute-start.2 = (bf16[2048,512]{1,0:T(8,128)(2,1)}, bf16[2048,512]{1,0:T(8,128)(2,1)}, u32[]{:S(2)}, u32[]{:S(2)}) collective-permute-start(bf16[2048,512]{1,0:T(8,128)(2,1)} %bitcast.119), channel_id=1, source_target_pairs={{0,4},{4,0},{8,12},{12,8},{16,20},{20,16},{24,28},{28,24},{1,5},{5... | collective-permute-start | bytes 6291464 | tf_op jit(solution)/shard_map/ppermute | solution.py:77
  164.1 4.9 %copy-start.22 = (bf16[32,512]{1,0:T(8,128)(2,1)}, bf16[32,512]{1,0:T(8,128)(2,1)S(1)}, u32[]{:S(2)}) copy-start(bf16[32,512]{1,0:T(8,128)(2,1)S(1)} %convolution_convert_fusion.9) | copy-start | bytes 98308
  170.9 4.9 %copy-start.9 = (f32[8,32,832]{2,1,0:T(8,128)}, f32[8,32,832]{2,1,0:T(8,128)S(1)}, u32[]{:S(2)}) copy-start(f32[8,32,832]{2,1,0:T(8,128)S(1)} %fusion.41) | copy-start | bytes 2555908
  175.8 2.5 copy-start.6
  178.3 5.5 %copy-start.23 = (bf16[32,512]{1,0:T(8,128)(2,1)}, bf16[32,512]{1,0:T(8,128)(2,1)S(1)}, u32[]{:S(2)}) copy-start(bf16[32,512]{1,0:T(8,128)(2,1)S(1)} %convolution_convert_fusion.8) | copy-start | bytes 98308
  185.8 4.9 %copy-start.4 = (f32[8,32,832]{2,1,0:T(8,128)}, f32[8,32,832]{2,1,0:T(8,128)S(1)}, u32[]{:S(2)}) copy-start(f32[8,32,832]{2,1,0:T(8,128)S(1)} %fusion.39) | copy-start | bytes 2555908
  190.6 0.9 copy-start.7
  199.8 4.6 %copy-start.21 = (s32[8,1,120]{2,1,0:T(1,128)S(1)}, s32[8,1,120]{2,1,0:T(1,128)}, u32[]{:S(2)}) copy-start(s32[8,1,120]{2,1,0:T(1,128)} %copy-done.20) | copy-start | bytes 11524
  199.8 4.7 %copy-start.19 = (s32[832]{0:T(1024)S(1)}, s32[832]{0:T(1024)}, u32[]{:S(2)}) copy-start(s32[832]{0:T(1024)} %copy-done.18) | copy-start | bytes 9988
  199.8 4.7 %copy-start.33 = (s32[32]{0:T(128)S(1)}, s32[32]{0:T(128)}, u32[]{:S(2)}) copy-start(s32[32]{0:T(128)} %copy-done.32) | copy-start | bytes 388
  202.9 29.5 %copy-start.28 = (f32[32]{0:T(128)}, f32[32]{0:T(128)S(1)}, u32[]{:S(2)}) copy-start(f32[32]{0:T(128)S(1)} %add_rsqrt_fusion) | copy-start | bytes 388
  228.6 0.8 copy-start.3
  232.6 3.7 %copy-start.30 = (f32[32]{0:T(128)}, f32[32]{0:T(128)S(1)}, u32[]{:S(2)}) copy-start(f32[32]{0:T(128)S(1)} %multiply_reduce_fusion.2) | copy-start | bytes 388
  232.6 5.0 %copy-start.8 = (bf16[832,512,1]{1,0,2:T(8,128)(2,1)S(1)}, bf16[832,512,1]{1,0,2:T(8,128)(2,1)}, u32[]{:S(2)}) copy-start(bf16[832,512,1]{1,0,2:T(8,128)(2,1)} %copy-done.7) | copy-start | bytes 2555908
  232.6 5.0 %copy-start.15 = (bf16[8,512]{1,0:T(8,128)(2,1)S(1)}, bf16[8,512]{1,0:T(8,128)(2,1)}, u32[]{:S(2)}) copy-start(bf16[8,512]{1,0:T(8,128)(2,1)} %copy-done.14) | copy-start | bytes 24580
  232.6 6.4 %copy-start.5 = (f32[8,32,832]{2,1,0:T(8,128)S(1)}, f32[8,32,832]{2,1,0:T(8,128)}, u32[]{:S(2)}) copy-start(f32[8,32,832]{2,1,0:T(8,128)} %copy-done.4) | copy-start | bytes 2555908
  236.9 0.6 copy-start.11
  251.2 3.6 %copy-start.29 = (f32[32]{0:T(128)S(1)}, f32[32]{0:T(128)}, u32[]{:S(2)}) copy-start(f32[32]{0:T(128)} %copy-done.28) | copy-start | bytes 388
  251.2 3.6 %copy-start.31 = (f32[32]{0:T(128)S(1)}, f32[32]{0:T(128)}, u32[]{:S(2)}) copy-start(f32[32]{0:T(128)} %copy-done.30) | copy-start | bytes 388
  254.7 1.5 copy-start.24
  254.7 3.8 %copy-start.17 = (pred[32,832]{1,0:T(32,128)(4,1)S(1)}, pred[32,832]{1,0:T(32,128)(4,1)}, u32[]{:S(2)}) copy-start(pred[32,832]{1,0:T(32,128)(4,1)} %broadcast_compare_fusion) | copy-start | bytes 79876
  258.6 4.0 %copy-start.10 = (f32[8,32,832]{2,1,0:T(8,128)S(1)}, f32[8,32,832]{2,1,0:T(8,128)}, u32[]{:S(2)}) copy-start(f32[8,32,832]{2,1,0:T(8,128)} %copy-done.9) | copy-start | bytes 2555908
  258.6 4.0 %copy-start.13 = (bf16[32,512]{1,0:T(8,128)(2,1)S(1)}, bf16[32,512]{1,0:T(8,128)(2,1)}, u32[]{:S(2)}) copy-start(bf16[32,512]{1,0:T(8,128)(2,1)} %get-tuple-element.21) | copy-start | bytes 98308
  258.6 4.0 %copy-start.16 = (bf16[8,512]{1,0:T(8,128)(2,1)S(1)}, bf16[8,512]{1,0:T(8,128)(2,1)}, u32[]{:S(2)}) copy-start(bf16[8,512]{1,0:T(8,128)(2,1)} %copy-done.14) | copy-start | bytes 24580
  262.6 6.7 %copy-start.41 = (bf16[832,512]{1,0:T(8,128)(2,1)S(1)}, bf16[832,512]{1,0:T(8,128)(2,1)}, u32[]{:S(2)}) copy-start(bf16[832,512]{1,0:T(8,128)(2,1)} %bitcast_convert_fusion.3) | copy-start | bytes 2555908
  269.3 6.4 %copy-start.40 = (bf16[832,512]{1,0:T(8,128)(2,1)S(1)}, bf16[832,512]{1,0:T(8,128)(2,1)}, u32[]{:S(2)}) copy-start(bf16[832,512]{1,0:T(8,128)(2,1)} %bitcast_convert_fusion.1) | copy-start | bytes 2555908
  275.7 6.4 %copy-start.12 = (bf16[32,512]{1,0:T(8,128)(2,1)S(1)}, bf16[32,512]{1,0:T(8,128)(2,1)}, u32[]{:S(2)}) copy-start(bf16[32,512]{1,0:T(8,128)(2,1)} %copy-done.11) | copy-start | bytes 98308
  295.8 4.9 %copy-start.35 = (f32[128]{0:T(128)S(1)}, f32[128]{0:T(128)}, u32[]{:S(2)}) copy-start(f32[128]{0:T(128)} %get-tuple-element.30) | copy-start | bytes 1540
  295.8 45.3 %copy-start.27 = (s32[640]{0:T(1024)S(1)}, s32[640]{0:T(1024)}, u32[]{:S(2)}) copy-start(s32[640]{0:T(1024)} %copy-done.26) | copy-start | bytes 7684
  295.8 45.3 %all-to-all-start.2 = ((bf16[8,104,2048]{2,1,0:T(8,128)(2,1)}), bf16[8,104,2048]{2,1,0:T(8,128)(2,1)}, u32[]{:S(2)}, u32[]{:S(2)}) async-start(bf16[8,104,2048]{2,1,0:T(8,128)(2,1)} %bitcast.106), calls=%async_computation.2 | async-start | bytes 6815744 | tf_op jit(solution)/shard_map/all_to_all | solution.py:188
  341.1 6.5 %copy-start.1 = (bf16[640,2048]{1,0:T(8,128)(2,1)S(1)}, bf16[640,2048]{1,0:T(8,128)(2,1)}, u32[]{:S(2)}) copy-start(bf16[640,2048]{1,0:T(8,128)(2,1)} %param.9) | copy-start | bytes 7864324
Sparse Core Ops, SparseCore 0:
  13.0 56.9 all-gather.11
  71.6 44.6 all-gather.13
  117.9 44.6 all-gather.15
  164.3 35.4 all-gather.9
  203.8 23.4 all-gather.17
where the time goes:
time: 355 us; the launch traced here: 354 us
  waiting for transfers between devices  171 us (48%)
  matrix products  107 us (30%)
  blocking collectives  23.3 us (7%)
  local copies, waits for them, and re-layouts  16.2 us (5%)
  starting transfers between devices  15 us (4%)
  between operations  15 us (4%)
  other arithmetic  6.61 us (2%)
    all_gather x3, waiting for transfers between devices, gather_half(): return lax.all_gather(piece, 'fsdp', axis=0, tiled=True)  71.3 us
    dot_general x10, matrix products, mmt(): lax.dot_general(a, b, (((1,), (1,)), ((), ())), preferred_element_type=F32)  45.4 us
    dot_general x15, matrix products, mm(): return jnp.dot(a, b, preferred_element_type=F32)  41.3 us
    all_to_all x1, waiting for transfers between devices, body(): lax.all_to_all(row_ct.astype(BF), 'dp', split_axis=0, concat_axis=0, tile...  39.8 us
    all_to_all x1, waiting for transfers between devices, body(): lax.all_to_all(send_rows, 'dp', split_axis=0, concat_axis=0, tiled=True)  29 us
    all_gather x1, blocking collectives, body(): out_piece = lax.all_gather(out_piece, 'fsdp', axis=1, tiled=True)  23.3 us
    all_gather x1, waiting for transfers between devices, body(): all_emb = lax.all_gather(unit.astype(BF), 'dp', axis=0)  22.1 us
    dot_general x4, matrix products, tmm(): lax.dot_general(a, b, (((0,), (0,)), ((), ())), preferred_element_type=F32)  17 us
  transfers between devices with their start and end apart: 11, of which 7 were waited for; matrix products, arithmetic and copies ran while one was open for 13% of the time, Pallas kernels for 0%

commit v1 on v0

v1 whole, which is shorter than its diff:
```python
import functools
import math

import jax
import jax.numpy as jnp
from jax import lax
from jax.experimental import pallas as pl
from jax.experimental.pallas import tpu as pltpu
from jax.sharding import PartitionSpec as P

HD = 64
EPSILON = 1e-06
FIXED = 2.0**20
BF = jnp.bfloat16
F32 = jnp.float32


def mm(a, b):
    return jnp.dot(a, b, preferred_element_type=F32)


def mmt(a, b):
    return lax.dot_general(a, b, (((1,), (1,)), ((), ())), preferred_element_type=F32)


def tmm(a, b):
    return lax.dot_general(a, b, (((0,), (0,)), ((), ())), preferred_element_type=F32)


def split3(x):
    hi = x.astype(BF)
    rest = x - hi.astype(F32)
    mid = rest.astype(BF)
    low = (rest - mid.astype(F32)).astype(BF)
    return jnp.concatenate([hi, mid, low], axis=0)


def exact_mm(x, emb):
    count = x.shape[0]
    parts = mm(split3(x), emb)
    return parts[:count] + parts[count : 2 * count] + parts[2 * count :]


def expand(x, head_mask):
    return (x[None] * head_mask.astype(x.dtype)).reshape(-1, x.shape[1])


def collapse(x, head_mask, rows):
    return jnp.sum(x.reshape(-1, rows, x.shape[1]) * head_mask, axis=0)


def move_kernel(
    dp_count,
    fs_count,
    capacity,
    rows_ref,
    qkv_ref,
    out_w_ref,
    got_ref,
    wq_ref,
    wkv_ref,
    wo_ref,
    z_send,
    z_recv,
    xy_send,
    xy_recv,
    sib_send,
    sib_recv,
    page_send,
    page_recv,
    local_sem,
):
    d = lax.axis_index("dp")
    f = lax.axis_index("fsdp")
    depth = qkv_ref.shape[1]
    hdim = qkv_ref.shape[2]
    cut = out_w_ref.shape[1]
    parity = d % 2
    chip = d // 2
    chips = dp_count // 2
    sibling = d + 1 - 2 * parity
    half_rows = depth // 2
    piece_rows = depth // dp_count
    half_out = hdim // 2
    piece_out = hdim // dp_count

    def put(src, dst, send, recv, dp, fsdp):
        return pltpu.make_async_remote_copy(
            src_ref=src,
            dst_ref=dst,
            send_sem=send,
            recv_sem=recv,
            device_id=(dp, fsdp),
            device_id_type=pl.DeviceIdType.MESH,
        )

    def at(owner, start, count):
        return pl.ds(pl.multiple_of(owner * depth + start, 16), count)

    def wo_at(owner, start, count):
        return wo_ref.at[
            pl.ds(pl.multiple_of(start, 16), count), pl.ds(pl.multiple_of(owner * cut, 128), cut)
        ]

    def regions(owner, c, piece):
        half = at(owner, c * half_rows, half_rows)
        small = at(owner, c * half_rows + piece * piece_rows, piece_rows)
        return dict(
            q=wq_ref.at[half, :],
            k=wkv_ref.at[half, pl.ds(0, hdim)],
            v=wkv_ref.at[small, pl.ds(hdim, hdim)],
            o=wo_at(owner, c * half_out + piece * piece_out, piece_out),
            v_half=wkv_ref.at[half, pl.ds(hdim, hdim)],
            o_half=wo_at(owner, c * half_out, half_out),
        )

    barrier = pltpu.get_barrier_semaphore()
    for k in range(1, fs_count):
        pl.semaphore_signal(
            barrier, inc=1, device_id=(d, (f + k) % fs_count), device_id_type=pl.DeviceIdType.MESH
        )
    for k in range(1, dp_count):
        pl.semaphore_signal(
            barrier, inc=1, device_id=((d + k) % dp_count, f), device_id_type=pl.DeviceIdType.MESH
        )
    pl.semaphore_wait(barrier, fs_count + dp_count - 2)

    sends = []

    def begin(copy):
        copy.start()
        sends.append(copy)

    half_src = pl.ds(pl.multiple_of(parity * half_rows, 16), half_rows)
    piece_src = pl.ds(
        pl.multiple_of(parity * half_rows + chip * piece_rows, 16), piece_rows
    )
    out_src = pl.ds(pl.multiple_of(parity * half_out + chip * piece_out, 16), piece_out)
    sources = dict(
        q=qkv_ref.at[0, half_src, :],
        k=qkv_ref.at[1, half_src, :],
        v=qkv_ref.at[2, piece_src, :],
        o=out_w_ref.at[out_src, :],
    )
    mine = regions(f, parity, chip)
    names = ("v", "o", "k", "q")
    for i, name in enumerate(names):
        for k in range(1, fs_count):
            begin(put(sources[name], mine[name], z_send.at[i, k], z_recv.at[i, k],
                      d, (f + k) % fs_count))
    for k in range(1, dp_count):
        to = (d + k) % dp_count
        begin(put(rows_ref.at[pl.ds(pl.multiple_of(to * capacity, 8), capacity), :],
                  got_ref.at[pl.ds(pl.multiple_of(d * capacity, 8), capacity), :],
                  page_send.at[k], page_recv.at[k], to, f))
    own = pl.ds(pl.multiple_of(d * capacity, 8), capacity)
    whole = at(f, 0, depth)
    locals_ = [
        pltpu.make_async_copy(rows_ref.at[own, :], got_ref.at[own, :], local_sem.at[0]),
        pltpu.make_async_copy(qkv_ref.at[0], wq_ref.at[whole, :], local_sem.at[1]),
        pltpu.make_async_copy(qkv_ref.at[1], wkv_ref.at[whole, pl.ds(0, hdim)], local_sem.at[2]),
        pltpu.make_async_copy(qkv_ref.at[2], wkv_ref.at[whole, pl.ds(hdim, hdim)], local_sem.at[3]),
        pltpu.make_async_copy(out_w_ref, wo_at(f, 0, hdim), local_sem.at[4]),
    ]
    for copy in locals_:
        copy.start()

    def arrived(region, send, recv):
        put(region, region, send, recv, sibling, f).wait_recv()

    for i, name in enumerate(("v", "o")):
        for k in range(1, fs_count):
            owner = (f + fs_count - k) % fs_count
            place = regions(owner, parity, chip)[name]
            arrived(place, z_send.at[i, k], z_recv.at[i, k])
            for j in range(1, chips):
                begin(put(place, place, xy_send.at[i, k, j], xy_recv.at[i, k, j],
                          2 * ((chip + j) % chips) + parity, f))
    for i, name in ((0, "v"), (1, "o"), (2, "k"), (3, "q")):
        for k in range(1, fs_count):
            owner = (f + fs_count - k) % fs_count
            if i < 2:
                for j in range(1, chips):
                    origin = (chip + chips - j) % chips
                    arrived(regions(owner, parity, origin)[name],
                            xy_send.at[i, k, j], xy_recv.at[i, k, j])
                place = regions(owner, parity, 0)[name + "_half"]
            else:
                place = regions(owner, parity, 0)[name]
                arrived(place, z_send.at[i, k], z_recv.at[i, k])
            begin(put(place, place, sib_send.at[i, k], sib_recv.at[i, k], sibling, f))
    for k in range(1, dp_count):
        origin = (d + dp_count - k) % dp_count
        arrived(got_ref.at[pl.ds(pl.multiple_of(origin * capacity, 8), capacity), :],
                page_send.at[k], page_recv.at[k])
    for i, name in ((0, "v_half"), (1, "o_half"), (2, "k"), (3, "q")):
        for k in range(1, fs_count):
            owner = (f + fs_count - k) % fs_count
            arrived(regions(owner, 1 - parity, 0)[name], sib_send.at[i, k], sib_recv.at[i, k])
    for copy in locals_:
        copy.wait()
    for copy in sends:
        copy.wait_send()


def move(send_rows, qkv_weight, out_weight, dp_count, fs_count, capacity):
    _, depth, hdim = qkv_weight.shape
    width = send_rows.shape[1]
    sem = pltpu.SemaphoreType.DMA
    any_spec = pl.BlockSpec(memory_space=pl.ANY)
    return pl.pallas_call(
        functools.partial(move_kernel, dp_count, fs_count, capacity),
        out_shape=(
            jax.ShapeDtypeStruct(send_rows.shape, BF),
            jax.ShapeDtypeStruct((depth * fs_count, hdim), BF),
            jax.ShapeDtypeStruct((depth * fs_count, 2 * hdim), BF),
            jax.ShapeDtypeStruct((hdim, width), BF),
        ),
        in_specs=[any_spec] * 3,
        out_specs=(any_spec,) * 4,
        scratch_shapes=[
            sem((4, fs_count)),
            sem((4, fs_count)),
            sem((2, fs_count, dp_count // 2)),
            sem((2, fs_count, dp_count // 2)),
            sem((4, fs_count)),
            sem((4, fs_count)),
            sem((dp_count,)),
            sem((dp_count,)),
            sem((5,)),
        ],
        compiler_params=pltpu.CompilerParams(collective_id=0, has_side_effects=True),
    )(send_rows, qkv_weight, out_weight)


def body(
    page_embed,
    page_slot,
    doc_ids,
    qkv_weight,
    out_weight,
    fig_slot,
    cap_slot,
    logit_scale,
    loss_cotangent,
):
    dp_count = lax.axis_size("dp")
    me = lax.axis_index("dp")
    fs_count = lax.axis_size("fsdp")
    row_count, width = page_embed.shape
    capacity = -(-(5 * row_count) // (4 * dp_count))
    capacity = -(-capacity // 16) * 16
    total = dp_count * capacity
    pair_count = fig_slot.shape[0]
    hdim = qkv_weight.shape[2]
    owner_idx = page_slot // row_count
    slot_idx = page_slot % row_count
    onehot = (owner_idx[:, None] == jnp.arange(dp_count)[None, :]).astype(jnp.int32)
    rank_idx = jnp.sum((jnp.cumsum(onehot, axis=0) - onehot) * onehot, axis=1)
    place_idx = owner_idx * capacity + rank_idx
    place = jnp.arange(total)[:, None] == place_idx[None, :]
    send_ids = jnp.sum(jnp.where(place, slot_idx[None, :] + 1, 0), axis=1) - 1
    fixed_ct = (loss_cotangent * FIXED).astype(jnp.int32)
    send_ints = jnp.concatenate(
        [
            send_ids.reshape(dp_count, capacity),
            jnp.broadcast_to(fixed_ct[None, :], (dp_count, pair_count)),
        ],
        axis=1,
    )
    recv_ints = lax.all_to_all(send_ints, "dp", split_axis=0, concat_axis=0, tiled=True)
    send_rows = mm(place.astype(BF), page_embed).astype(BF)
    rows, w_q, w_kv, w_out = move(
        send_rows, qkv_weight, out_weight, dp_count, fs_count, capacity
    )

    ids = recv_ints[:, :capacity].reshape(-1)
    group_ct = recv_ints[:, capacity:].reshape(-1).astype(F32) * (1.0 / FIXED)
    doc_row = doc_ids[0]
    slot_range = jnp.arange(row_count)
    row_docs = (
        jnp.sum(jnp.where(ids[:, None] == slot_range[None, :], doc_row[None, :] + 1, 0), axis=1) - 1
    )
    slots = jnp.concatenate([fig_slot, cap_slot])
    slot_docs = jnp.sum(jnp.where(slots[:, None] == slot_range[None, :], doc_row[None, :], 0), axis=1)
    picked = (slots[:, None] == ids[None, :]).astype(BF)
    same_doc = slot_docs[:, None] == row_docs[None, :]
    pick_count = slots.shape[0]

    picked_rows = mm(picked, rows).astype(BF)
    scale = 1.0 / math.sqrt(HD)
    heads = hdim // HD
    head_mask = (
        jnp.arange(hdim)[None, None, :] // HD == jnp.arange(heads)[:, None, None]
    ).astype(F32)

    key_value = mm(rows, w_kv).astype(BF)
    key, value = key_value[:, :hdim], key_value[:, hdim:]
    query = expand(mm(picked_rows, w_q).astype(BF), head_mask)
    scores = mmt(query, key).reshape(heads, pick_count, total) * scale
    weights = jnp.exp(jnp.where(same_doc[None], scores, -1e30))
    prob = weights / jnp.sum(weights, axis=2, keepdims=True)
    prob_b = prob.astype(BF).reshape(heads * pick_count, total)
    mixed = collapse(mm(prob_b, value), head_mask, pick_count).astype(BF)
    attn_out = mm(mixed, w_out)

    vec = picked_rows.astype(F32) + attn_out
    inv = lax.rsqrt(jnp.sum(vec * vec, axis=1, keepdims=True) + EPSILON)
    unit = vec * inv
    all_fig = lax.all_gather(unit[:pair_count].astype(BF), "dp", axis=0, tiled=True)
    all_cap = lax.all_gather(unit[pair_count:].astype(BF), "dp", axis=0, tiled=True)
    logit_mult = logit_scale[0]
    logits = logit_mult * mmt(all_fig, all_cap)
    row_lse = jnp.log(jnp.sum(jnp.exp(logits), axis=1))
    col_lse = jnp.log(jnp.sum(jnp.exp(logits), axis=0))
    group_pairs = logits.shape[0]
    eye = jnp.arange(group_pairs)[:, None] == jnp.arange(group_pairs)[None, :]
    diag = jnp.sum(jnp.where(eye, logits, 0.0), axis=1)
    eye = eye.astype(F32)
    all_loss = 0.5 * (row_lse - diag) + 0.5 * (col_lse - diag)
    pair_loss = lax.dynamic_slice_in_dim(all_loss, me * pair_count, pair_count, 0)
    coef = 0.5 * group_ct[:, None] * (jnp.exp(logits - row_lse[:, None]) - eye) + 0.5 * (
        jnp.exp(logits - col_lse[None, :]) - eye
    ) * group_ct[None, :]
    coef_f = lax.dynamic_slice_in_dim(coef, me * pair_count, pair_count, 0)
    coef_c = lax.dynamic_slice_in_dim(coef.T, me * pair_count, pair_count, 0)
    grad = logit_mult * jnp.concatenate(
        [exact_mm(coef_f, all_cap), exact_mm(coef_c, all_fig)], axis=0
    )
    dvec = inv * (grad - unit * jnp.sum(unit * grad, axis=1, keepdims=True))

    dmix = expand(mmt(dvec.astype(BF), w_out).astype(BF), head_mask)
    dprob = mmt(dmix, value).reshape(heads, pick_count, total)
    dscore = prob * (dprob - jnp.sum(dprob * prob, axis=2, keepdims=True)) * scale
    dscore = dscore.astype(BF).reshape(heads * pick_count, total)
    dquery = collapse(mm(dscore, key), head_mask, pick_count).astype(BF)
    picked_ct = dvec + mmt(dquery, w_q)
    dkey_value = jnp.concatenate(
        [tmm(dscore, query).astype(BF), tmm(prob_b, dmix).astype(BF)], axis=1
    )
    ct_hi = picked_ct.astype(BF)
    ct_lo = (picked_ct - ct_hi.astype(F32)).astype(BF)
    row_ct = mmt(dkey_value, w_kv) + tmm(
        jnp.concatenate([picked, picked], axis=0), jnp.concatenate([ct_hi, ct_lo], axis=0)
    )
    home = lax.all_to_all(row_ct.astype(BF), "dp", split_axis=0, concat_axis=0, tiled=True)
    page_grad = tmm(place.astype(BF), home).astype(BF)
    return (page_grad, pair_loss)


def solution(mesh):
    return jax.shard_map(
        body,
        mesh=mesh,
        in_specs=(
            P(("dp", "fsdp"), None),
            P(("dp", "fsdp")),
            P(("dp", "fsdp"), None),
            P(None, "fsdp", None),
            P(None, "fsdp"),
            P(("dp", "fsdp")),
            P(("dp", "fsdp")),
            P(),
            P(("dp", "fsdp")),
        ),
        out_specs=(P(("dp", "fsdp"), None), P(("dp", "fsdp"))),
        check_vma=False,
    )
```

time: 355 us -> 309 us (0.87)
  Pallas kernels: 0 us -> 147 us
  waiting for transfers between devices: 171 us -> 42.7 us
  matrix products: 107 us -> 76.8 us
  local copies, waits for them, and re-layouts: 16.2 us -> 2.25 us
  between operations: 15 us -> 1.66 us
  starting transfers between devices: 15 us -> 10 us
    pallas_call x0 -> x1, Pallas kernels: none -> 147 us  [move(): pl.pallas_call(functools.partial(move_kernel, dp_count, fs_count, capacit...]
    all_gather x5 -> x0, waiting for transfers between devices: 102 us -> none  [the longest x3 71.3 us: gather_half(): return lax.all_gather(piece, 'fsdp', axis=0, tiled=True)]
    all_to_all x1 -> x0, waiting for transfers between devices: 29 us -> none  [body(): lax.all_to_all(send_rows, 'dp', split_axis=0, concat_axis=0, tiled=True)]
    dot_general x10 -> x5, matrix products: 45.4 us -> 19.2 us  [mmt(): lax.dot_general(a, b, (((1,), (1,)), ((), ())), preferred_element_type=F32)]
    dynamic_slice x4 -> x0, local copies, waits for them, and re-layouts: 6.59 us -> none  [the longest x3 5.67 us: gather_half(): lax.dynamic_slice_in_dim(qkv_weight[index], half * half_width, half_width...]
    dot_general x15 -> x9, matrix products: 41.3 us -> 35.2 us  [mm(): return jnp.dot(a, b, preferred_element_type=F32)]
    slice x4 -> x3, local copies, waits for them, and re-layouts: 5.23 us -> 0.22 us  [the longest x1 3.74 us: gather_half(): qkv_weight[index]]
    all_to_all x1 -> x0, starting transfers between devices: 4.63 us -> none  [body(): lax.all_to_all(send_rows, 'dp', split_axis=0, concat_axis=0, tiled=True)]
  transfers between devices with their start and end apart: 11 -> 2, of which waited for: 7 -> 1; matrix products, arithmetic and copies ran while one was open for 13% -> 6% of each run, Pallas kernels for 0% -> 48%
where the time goes in v1:
time: 309 us
  Pallas kernels  147 us (48%)
  matrix products  76.8 us (25%)
  waiting for transfers between devices  42.7 us (14%)
  blocking collectives  21.3 us (7%)
  starting transfers between devices  10 us (3%)
  other arithmetic  6.89 us (2%)
    pallas_call x1, Pallas kernels, move(): pl.pallas_call(functools.partial(move_kernel, dp_count, fs_count, capacit...  147 us
    all_to_all x1, waiting for transfers between devices, body(): lax.all_to_all(row_ct.astype(BF), 'dp', split_axis=0, concat_axis=0, tile...  42.7 us
    dot_general x9, matrix products, mm(): return jnp.dot(a, b, preferred_element_type=F32)  35.2 us
    dot_general x5, matrix products, mmt(): lax.dot_general(a, b, (((1,), (1,)), ((), ())), preferred_element_type=F32)  19.2 us
    dot_general x4, matrix products, tmm(): lax.dot_general(a, b, (((0,), (0,)), ((), ())), preferred_element_type=F32)  18.1 us
    all_gather x1, blocking collectives, body(): lax.all_gather(unit[pair_count:].astype(BF), 'dp', axis=0, tiled=True)  11 us
    all_gather x1, blocking collectives, body(): lax.all_gather(unit[:pair_count].astype(BF), 'dp', axis=0, tiled=True)  10.4 us
  transfers between devices with their start and end apart: 2, of which 1 were waited for; matrix products, arithmetic and copies ran while one was open for 6% of the time, Pallas kernels for 48%

profile of v1, /device:TPU:0, one launch (start us, length us, event | category | flops | bytes accessed | tf_op | source)
XLA Modules:
  0.0 308.7 jit_solution(17141398735123232015)
XLA Ops:
  0.6 0.0 copy-start
  0.6 0.9 add_select_fusion.2
  1.5 1.4 reduce-window.6
  2.9 0.1 slice.58
  3.0 0.1 copy.28
  3.1 0.2 reduce-window.9
  3.3 0.1 copy.29
  3.4 0.1 fusion.49
  3.5 0.7 fusion.64
  4.2 0.3 select_reduce_fusion.1
  4.5 0.1 sub.86
  4.6 0.7 multiply_convert_fusion.2
  5.3 0.1 pad.15.clone
  5.3 0.6 pad_add_fusion
  5.9 5.2 %all-to-all-start = ((s32[8,1,128]{2,1,0:T(1,128)}), s32[8,1,128]{2,1,0:T(1,128)S(1)}, u32[]{:S(2)}, u32[]{:S(2)}) async-start(s32[8,1,128]{2,1,0:T(1,128)} %bitcast.4), calls=%async_computation | async-start | bytes 8192 | tf_op jit(solution)/shard_map/all_to_all | solution.py:271
  11.1 0.0 copy-start.13
  11.1 0.0 copy-start.15
  11.2 0.0 copy-start.16
  11.2 4.5 %convolution_convert_fusion.rows_ref = bf16[896,2048]{1,0:T(8,128)(2,1)} fusion(bf16[640,2048]{1,0:T(8,128)(2,1)S(1)} %copy-done, s32[640]{0:T(1024)S(1)} %get-tuple-element.28), kind=kOutput, calls=%fused_computation.8 | convolution fusion | flops 2351218688 | bytes 6294016 | tf_op jit(solution)/shard_map/dot_general | solution.py:19
  15.7 0.0 copy-done.15
  15.7 0.1 pad_add_fusion.1
  15.8 147.1 %shard_map.104 = (bf16[896,2048]{1,0:T(8,128)(2,1)}, bf16[2048,1024]{1,0:T(8,128)(2,1)}, bf16[2048,2048]{1,0:T(8,128)(2,1)}, bf16[1024,2048]{1,0:T(8,128)(2,1)}) custom-call(bf16[896,2048]{1,0:T(8,128)(2,1)} %convolution_convert_fusion.rows_ref, bf16[3,512,1024]{2,1,0:T(8,128)(2,1)} %qkv_ref.1, bf16[1024,512]{1,0:T(8,128)(2,1)} %out_w_ref.1), custom_call_target="tpu_custom_call" | custom-call | tf_op jit(solution)/shard_map/pallas_call | solution.py:211
  162.9 13.1 %convolution_convert_fusion.1 = bf16[896,2048]{1,0:T(8,128)(2,1)} fusion(bf16[896,2048]{1,0:T(8,128)(2,1)} %get-tuple-element.6, bf16[2048,2048]{1,0:T(8,128)(2,1)} %get-tuple-element.8), kind=kOutput, calls=%fused_computation.9 | convolution fusion | flops 7518027776 | bytes 15728640 | tf_op jit(solution)/shard_map/dot_general | solution.py:19
  176.0 0.2 select_reduce_fusion.2
  176.8 0.0 all-to-all-done
  176.8 0.1 convert_multiply_fusion
  176.9 0.1 eq.174
  177.0 2.8 convolution_convert_fusion.3
  179.8 0.5 select_reduce_fusion
  180.3 3.0 convolution_convert_fusion.5
  183.3 0.0 copy-start.3
  183.3 0.1 broadcast_compare_fusion.1
  183.4 4.2 %fusion.20 = f32[16,32,896]{2,1,0:T(8,128)} fusion(bf16[896,2048]{1,0:T(8,128)(2,1)} %convolution_convert_fusion.1, pred[32,896]{1,0:T(8,128)(4,1)S(1)} %broadcast_compare_fusion.1, bf16[16,1024]{1,0:T(8,128)(2,1)S(1)} %get-tuple-element.25, bf16[32,1024]{1,0:T(8,128)(2,1)S(1)} %convolution_convert_fusion.5), kind=kOutput, calls=%fused_computation.37 | convolution fusion | flops 941426048 | bytes 3796992 | tf_op jit(solution)/shard_map/div | solution.py:302
  187.6 3.5 %multiply_reduce_fusion.1 = bf16[32,1024]{1,0:T(8,128)(2,1)S(1)} fusion(bf16[896,2048]{1,0:T(8,128)(2,1)} %convolution_convert_fusion.1, f32[16,1024]{1,0:T(8,128)S(1)} %get-tuple-element.26, f32[16,32,896]{2,1,0:T(8,128)} %fusion.20), kind=kOutput, calls=%fused_computation.19 | convolution fusion | flops 940998656 | bytes 3801088 | tf_op jit(solution)/shard_map/dot_general | solution.py:19
  191.0 0.9 multiply_reduce_fusion.4
  192.0 0.1 multiply_convert_fusion.1
  192.1 10.4 %all_gather.6 = bf16[128,2048]{1,0:T(8,128)(2,1)S(1)} all-gather(bf16[16,2048]{1,0:T(8,128)(2,1)S(1)} %get-tuple-element.24), channel_id=1, replica_groups=mesh['dp'=8,'fsdp'=4] {'dp'}, dimensions={0}, use_global_device_ids=true | all-gather | bytes 589824 | tf_op jit(solution)/shard_map/all_gather | solution.py:310
  202.5 11.0 %all_gather.7 = bf16[128,2048]{1,0:T(8,128)(2,1)} all-gather(bf16[16,2048]{1,0:T(8,128)(2,1)S(1)} %get-tuple-element.23), channel_id=1, replica_groups=mesh['dp'=8,'fsdp'=4] {'dp'}, dimensions={0}, use_global_device_ids=true | all-gather | bytes 589824 | tf_op jit(solution)/shard_map/all_gather | solution.py:311
  213.4 0.1 mul.175
  213.5 1.4 select_reduce_fusion.3
  215.0 0.5 add_multiply_fusion
  215.5 0.1 fusion.41
  215.6 0.1 convert_subtract_fusion.2
  215.7 0.7 copy.31
  216.4 0.1 copy.32
  216.4 0.1 copy.33
  216.5 1.3 fusion.51
  217.8 0.9 fusion.57
  218.8 0.2 multiply_reduce_fusion.3
  219.0 3.7 %convolution_convert_fusion.4 = bf16[32,1024]{1,0:T(8,128)(2,1)S(1)} fusion(bf16[1024,2048]{1,0:T(8,128)(2,1)} %get-tuple-element.9, f32[32,2048]{1,0:T(8,128)S(1)} %get-tuple-element.35, f32[16,2048]{1,0:T(8,128)S(1)} %get-tuple-element.37, f32[16,2048]{1,0:T(8,128)S(1)} %get-tuple-element.38, f32[32]{0:T(128)S(1)} %multiply_reduce_fusion.3, f32[]{:T(128)} %bitcast.60, ...), kind=kOutput, calls=%fused_computation.33 | convolution fusion | flops 134709248 | bytes 4784388 | tf_op jit(solution)/shard_map/dot_general | solution.py:23
  222.7 0.0 copy-done.17
  222.7 2.6 fusion.9
  225.3 5.3 %multiply_reduce_fusion = bf16[32,1024]{1,0:T(8,128)(2,1)S(1)} fusion(bf16[896,2048]{1,0:T(8,128)(2,1)} %convolution_convert_fusion.1, f32[16,1024]{1,0:T(8,128)S(1)} %copy-done.6, f32[16,32,896]{2,1,0:T(8,128)} %fusion.20, f32[16,32,896]{2,1,0:T(8,128)} %fusion.9), kind=kOutput, calls=%fused_computation.18 | convolution fusion | flops 942835072 | bytes 9306112 | tf_op jit(solution)/shard_map/dot_general | solution.py:19
  230.6 5.8 %bitcast_convert_fusion.1 = bf16[896,1024]{1,0:T(8,128)(2,1)} fusion(f32[16,32,896]{2,1,0:T(8,128)} %fusion.20, f32[16,32,896]{2,1,0:T(8,128)} %fusion.9, bf16[16,1024]{1,0:T(8,128)(2,1)S(1)} %get-tuple-element.25, bf16[32,1024]{1,0:T(8,128)(2,1)S(1)} %copy-done.4), kind=kOutput, calls=%fused_computation.7 | convolution fusion | flops 943261056 | bytes 5603328 | tf_op jit(solution)/shard_map/dot_general | solution.py:27
  236.4 2.8 bitcast_convert_fusion
  239.3 0.1 broadcast_compare_fusion
  239.4 1.4 subtract_convert_fusion
  240.7 0.1 copy-done.18
  240.9 10.2 %fusion.1 = f32[896,2048]{1,0:T(8,128)S(1)} fusion(bf16[2048,2048]{1,0:T(8,128)(2,1)} %get-tuple-element.8, bf16[896,1024]{1,0:T(8,128)(2,1)S(1)} %bitcast_convert_fusion, bf16[896,1024]{1,0:T(8,128)(2,1)S(1)} %copy-done.18), kind=kOutput, calls=%fused_computation.2 | convolution fusion | flops 7523532800 | bytes 19398656 | tf_op jit(solution)/shard_map/dot_general | solution.py:23
  251.1 3.0 add_convert_fusion
  254.1 4.8 %all-to-all-start.1 = ((bf16[8,112,2048]{2,1,0:T(8,128)(2,1)}), bf16[8,112,2048]{2,1,0:T(8,128)(2,1)}, u32[]{:S(2)}, u32[]{:S(2)}) async-start(bf16[8,112,2048]{2,1,0:T(8,128)(2,1)} %bitcast.62), calls=%async_computation.1 | async-start | bytes 7340032 | tf_op jit(solution)/shard_map/all_to_all | solution.py:346
  259.0 0.6 dynamic_slice.11
  259.6 42.7 %all-to-all-done.1 = bf16[8,112,2048]{2,1,0:T(8,128)(2,1)} async-done(((bf16[8,112,2048]{2,1,0:T(8,128)(2,1)}), bf16[8,112,2048]{2,1,0:T(8,128)(2,1)}, u32[]{:S(2)}, u32[]{:S(2)}) %all-to-all-start.1) | async-done | bytes 3670048 | tf_op jit(solution)/shard_map/all_to_all | solution.py:346
  302.3 6.5 %convolution_convert_fusion.2 = bf16[640,2048]{1,0:T(8,128)(2,1)} fusion(bf16[896,2048]{1,0:T(8,128)(2,1)} %bitcast.13, s32[640]{0:T(1024)S(1)} %copy-done.8), kind=kOutput, calls=%fused_computation.10 | convolution fusion | flops 2350694400 | bytes 6294016 | tf_op jit(solution)/shard_map/dot_general | solution.py:27
  (40 shorter events, 0.2 us)
Async XLA Ops:
  0.6 10.5 %copy-start = (bf16[640,2048]{1,0:T(8,128)(2,1)S(1)}, bf16[640,2048]{1,0:T(8,128)(2,1)}, u32[]{:S(2)}) copy-start(bf16[640,2048]{1,0:T(8,128)(2,1)} %param.9) | copy-start | bytes 7864324
  4.2 6.9 %copy-start.7 = (s32[640]{0:T(1024)}, s32[640]{0:T(1024)S(1)}, u32[]{:S(2)}) copy-start(s32[640]{0:T(1024)S(1)} %get-tuple-element.28) | copy-start | bytes 7684
  5.9 170.9 %all-to-all-start = ((s32[8,1,128]{2,1,0:T(1,128)}), s32[8,1,128]{2,1,0:T(1,128)S(1)}, u32[]{:S(2)}, u32[]{:S(2)}) async-start(s32[8,1,128]{2,1,0:T(1,128)} %bitcast.4), calls=%async_computation | async-start | bytes 8192 | tf_op jit(solution)/shard_map/all_to_all | solution.py:271
  11.1 4.5 %copy-start.13 = (s32[1,640]{1,0:T(1,128)S(1)}, s32[1,640]{1,0:T(1,128)}, u32[]{:S(2)}) copy-start(s32[1,640]{1,0:T(1,128)} %param.11) | copy-start | bytes 7684
  11.1 4.5 %copy-start.15 = (s32[16]{0:T(128)S(1)}, s32[16]{0:T(128)}, u32[]{:S(2)}) copy-start(s32[16]{0:T(128)} %param.15) | copy-start | bytes 196
  11.2 4.5 %copy-start.16 = (s32[16]{0:T(128)S(1)}, s32[16]{0:T(128)}, u32[]{:S(2)}) copy-start(s32[16]{0:T(128)} %param.14) | copy-start | bytes 196
  15.7 171.9 %copy-start.5 = (f32[16,1024]{1,0:T(8,128)}, f32[16,1024]{1,0:T(8,128)S(1)}, u32[]{:S(2)}) copy-start(f32[16,1024]{1,0:T(8,128)S(1)} %get-tuple-element.26) | copy-start | bytes 196612
  15.8 161.2 %copy-start.11 = (s32[32]{0:T(128)}, s32[32]{0:T(128)S(1)}, u32[]{:S(2)}) copy-start(s32[32]{0:T(128)S(1)} %pad_add_fusion.1) | copy-start | bytes 388
  183.3 4.3 %copy-start.3 = (bf16[32,1024]{1,0:T(8,128)(2,1)}, bf16[32,1024]{1,0:T(8,128)(2,1)S(1)}, u32[]{:S(2)}) copy-start(bf16[32,1024]{1,0:T(8,128)(2,1)S(1)} %convolution_convert_fusion.5) | copy-start | bytes 196612
  187.6 3.5 %copy-start.2 = (bf16[1024,2048]{1,0:T(8,128)(2,1)S(1)}, bf16[1024,2048]{1,0:T(8,128)(2,1)}, u32[]{:S(2)}) copy-start(bf16[1024,2048]{1,0:T(8,128)(2,1)} %get-tuple-element.9) | copy-start | bytes 12582916
  192.0 23.6 %copy-start.9 = (f32[32]{0:T(128)}, f32[32]{0:T(128)S(1)}, u32[]{:S(2)}) copy-start(f32[32]{0:T(128)S(1)} %add_rsqrt_fusion) | copy-start | bytes 388
  216.4 2.4 copy-start.10
  219.0 3.7 %copy-start.17 = (bf16[896,2048]{1,0:T(8,128)(2,1)S(1)}, bf16[896,2048]{1,0:T(8,128)(2,1)}, u32[]{:S(2)}) copy-start(bf16[896,2048]{1,0:T(8,128)(2,1)} %convolution_convert_fusion.1) | copy-start | bytes 11010052
  222.7 2.6 copy-start.6
  225.3 5.3 %copy-start.4 = (bf16[32,1024]{1,0:T(8,128)(2,1)S(1)}, bf16[32,1024]{1,0:T(8,128)(2,1)}, u32[]{:S(2)}) copy-start(bf16[32,1024]{1,0:T(8,128)(2,1)} %copy-done.3) | copy-start | bytes 196612
  236.4 2.8 copy-start.12
  236.4 2.9 copy-start.1
  239.4 1.5 copy-start.18
  254.1 4.9 %copy-start.14 = (f32[128]{0:T(128)S(1)}, f32[128]{0:T(128)}, u32[]{:S(2)}) copy-start(f32[128]{0:T(128)} %get-tuple-element.31) | copy-start | bytes 1540
  254.1 48.1 %copy-start.8 = (s32[640]{0:T(1024)S(1)}, s32[640]{0:T(1024)}, u32[]{:S(2)}) copy-start(s32[640]{0:T(1024)} %copy-done.7) | copy-start | bytes 7684
  254.1 48.1 %all-to-all-start.1 = ((bf16[8,112,2048]{2,1,0:T(8,128)(2,1)}), bf16[8,112,2048]{2,1,0:T(8,128)(2,1)}, u32[]{:S(2)}, u32[]{:S(2)}) async-start(bf16[8,112,2048]{2,1,0:T(8,128)(2,1)} %bitcast.62), calls=%async_computation.1 | async-start | bytes 7340032 | tf_op jit(solution)/shard_map/all_to_all | solution.py:346

commit v2 on v1

--- a/solution.py
+++ b/solution.py
@@ -56,10 +56,12 @@
     rows_ref,
     qkv_ref,
     out_w_ref,
+    ints_ref,
     got_ref,
     wq_ref,
     wkv_ref,
     wo_ref,
+    got_ints_ref,
     z_send,
     z_recv,
     xy_send,
@@ -68,6 +70,8 @@
     sib_recv,
     page_send,
     page_recv,
+    ints_send,
+    ints_recv,
     local_sem,
 ):
     d = lax.axis_index("dp")
@@ -107,7 +111,8 @@
         small = at(owner, c * half_rows + piece * piece_rows, piece_rows)
         return dict(
             q=wq_ref.at[half, :],
-            k=wkv_ref.at[half, pl.ds(0, hdim)],
+            k=wkv_ref.at[small, pl.ds(0, hdim)],
+            k_half=wkv_ref.at[half, pl.ds(0, hdim)],
             v=wkv_ref.at[small, pl.ds(hdim, hdim)],
             o=wo_at(owner, c * half_out + piece * piece_out, piece_out),
             v_half=wkv_ref.at[half, pl.ds(hdim, hdim)],
@@ -138,12 +143,12 @@
     out_src = pl.ds(pl.multiple_of(parity * half_out + chip * piece_out, 16), piece_out)
     sources = dict(
         q=qkv_ref.at[0, half_src, :],
-        k=qkv_ref.at[1, half_src, :],
+        k=qkv_ref.at[1, piece_src, :],
         v=qkv_ref.at[2, piece_src, :],
         o=out_w_ref.at[out_src, :],
     )
     mine = regions(f, parity, chip)
-    names = ("v", "o", "k", "q")
+    names = ("k", "v", "o", "q")
     for i, name in enumerate(names):
         for k in range(1, fs_count):
             begin(put(sources[name], mine[name], z_send.at[i, k], z_recv.at[i, k],
@@ -153,6 +158,7 @@
         begin(put(rows_ref.at[pl.ds(pl.multiple_of(to * capacity, 8), capacity), :],
                   got_ref.at[pl.ds(pl.multiple_of(d * capacity, 8), capacity), :],
                   page_send.at[k], page_recv.at[k], to, f))
+        begin(put(ints_ref.at[to], got_ints_ref.at[d], ints_send.at[k], ints_recv.at[k], to, f))
     own = pl.ds(pl.multiple_of(d * capacity, 8), capacity)
     whole = at(f, 0, depth)
     locals_ = [
@@ -161,6 +167,7 @@
         pltpu.make_async_copy(qkv_ref.at[1], wkv_ref.at[whole, pl.ds(0, hdim)], local_sem.at[2]),
         pltpu.make_async_copy(qkv_ref.at[2], wkv_ref.at[whole, pl.ds(hdim, hdim)], local_sem.at[3]),
         pltpu.make_async_copy(out_w_ref, wo_at(f, 0, hdim), local_sem.at[4]),
+        pltpu.make_async_copy(ints_ref.at[d], got_ints_ref.at[d], local_sem.at[5]),
     ]
     for copy in locals_:
         copy.start()
@@ -168,7 +175,7 @@
     def arrived(region, send, recv):
         put(region, region, send, recv, sibling, f).wait_recv()
 
-    for i, name in enumerate(("v", "o")):
+    for i, name in enumerate(names[:3]):
         for k in range(1, fs_count):
             owner = (f + fs_count - k) % fs_count
             place = regions(owner, parity, chip)[name]
@@ -176,10 +183,10 @@
             for j in range(1, chips):
                 begin(put(place, place, xy_send.at[i, k, j], xy_recv.at[i, k, j],
                           2 * ((chip + j) % chips) + parity, f))
-    for i, name in ((0, "v"), (1, "o"), (2, "k"), (3, "q")):
+    for i, name in enumerate(names):
         for k in range(1, fs_count):
             owner = (f + fs_count - k) % fs_count
-            if i < 2:
+            if i < 3:
                 for j in range(1, chips):
                     origin = (chip + chips - j) % chips
                     arrived(regions(owner, parity, origin)[name],
@@ -193,7 +200,8 @@
         origin = (d + dp_count - k) % dp_count
         arrived(got_ref.at[pl.ds(pl.multiple_of(origin * capacity, 8), capacity), :],
                 page_send.at[k], page_recv.at[k])
-    for i, name in ((0, "v_half"), (1, "o_half"), (2, "k"), (3, "q")):
+        arrived(got_ints_ref.at[origin], ints_send.at[k], ints_recv.at[k])
+    for i, name in enumerate(("k_half", "v_half", "o_half", "q")):
         for k in range(1, fs_count):
             owner = (f + fs_count - k) % fs_count
             arrived(regions(owner, 1 - parity, 0)[name], sib_send.at[i, k], sib_recv.at[i, k])
@@ -203,7 +211,7 @@
         copy.wait_send()
 
 
-def move(send_rows, qkv_weight, out_weight, dp_count, fs_count, capacity):
+def move(send_rows, qkv_weight, out_weight, ints, dp_count, fs_count, capacity):
     _, depth, hdim = qkv_weight.shape
     width = send_rows.shape[1]
     sem = pltpu.SemaphoreType.DMA
@@ -215,22 +223,66 @@
             jax.ShapeDtypeStruct((depth * fs_count, hdim), BF),
             jax.ShapeDtypeStruct((depth * fs_count, 2 * hdim), BF),
             jax.ShapeDtypeStruct((hdim, width), BF),
+            jax.ShapeDtypeStruct(ints.shape, jnp.int32),
         ),
-        in_specs=[any_spec] * 3,
-        out_specs=(any_spec,) * 4,
+        in_specs=[any_spec] * 4,
+        out_specs=(any_spec,) * 5,
         scratch_shapes=[
             sem((4, fs_count)),
             sem((4, fs_count)),
-            sem((2, fs_count, dp_count // 2)),
-            sem((2, fs_count, dp_count // 2)),
+            sem((3, fs_count, dp_count // 2)),
+            sem((3, fs_count, dp_count // 2)),
             sem((4, fs_count)),
             sem((4, fs_count)),
             sem((dp_count,)),
             sem((dp_count,)),
-            sem((5,)),
+            sem((dp_count,)),
+            sem((dp_count,)),
+            sem((6,)),
         ],
         compiler_params=pltpu.CompilerParams(collective_id=0, has_side_effects=True),
-    )(send_rows, qkv_weight, out_weight)
+    )(send_rows, qkv_weight, out_weight, ints)
+
+
+def share_kernel(dp_count, emb_ref, all_ref, send, recv):
+    d = lax.axis_index("dp")
+    f = lax.axis_index("fsdp")
+    barrier = pltpu.get_barrier_semaphore()
+    for k in range(1, dp_count):
+        pl.semaphore_signal(
+            barrier, inc=1, device_id=((d + k) % dp_count, f), device_id_type=pl.DeviceIdType.MESH
+        )
+    pl.semaphore_wait(barrier, dp_count - 1)
+
+    def put(place, k, to):
+        return pltpu.make_async_remote_copy(
+            src_ref=emb_ref,
+            dst_ref=all_ref.at[place],
+            send_sem=send.at[k],
+            recv_sem=recv.at[k],
+            device_id=(to, f),
+            device_id_type=pl.DeviceIdType.MESH,
+        )
+
+    copies = [put(d, k, (d + k) % dp_count) for k in range(1, dp_count)]
+    for copy in copies:
+        copy.start()
+    all_ref[d] = emb_ref[...]
+    for k in range(1, dp_count):
+        put((d + dp_count - k) % dp_count, k, (d + k) % dp_count).wait_recv()
+    for copy in copies:
+        copy.wait_send()
+
+
+def share(emb, dp_count):
+    return pl.pallas_call(
+        functools.partial(share_kernel, dp_count),
+        out_shape=jax.ShapeDtypeStruct((dp_count,) + emb.shape, emb.dtype),
+        in_specs=[pl.BlockSpec(memory_space=pltpu.VMEM)],
+        out_specs=pl.BlockSpec(memory_space=pltpu.VMEM),
+        scratch_shapes=[pltpu.SemaphoreType.DMA((dp_count,)), pltpu.SemaphoreType.DMA((dp_count,))],
+        compiler_params=pltpu.CompilerParams(collective_id=1, has_side_effects=True),
+    )(emb)
 
 
 def body(
@@ -268,14 +320,16 @@
         ],
         axis=1,
     )
-    recv_ints = lax.all_to_all(send_ints, "dp", split_axis=0, concat_axis=0, tiled=True)
+    send_ints = jnp.pad(send_ints, ((0, 0), (0, -send_ints.shape[1] % 128)))
+    send_ints = jnp.broadcast_to(send_ints[:, None], (dp_count, 8, send_ints.shape[1]))
     send_rows = mm(place.astype(BF), page_embed).astype(BF)
-    rows, w_q, w_kv, w_out = move(
-        send_rows, qkv_weight, out_weight, dp_count, fs_count, capacity
-    )
+    rows, w_q, w_kv, w_out, recv_ints = move(
+        send_rows, qkv_weight, out_weight, send_ints, dp_count, fs_count, capacity
+    )
+    recv_ints = recv_ints[:, 0]
 
     ids = recv_ints[:, :capacity].reshape(-1)
-    group_ct = recv_ints[:, capacity:].reshape(-1).astype(F32) * (1.0 / FIXED)
+    group_ct = recv_ints[:, capacity : capacity + pair_count].reshape(-1).astype(F32) * (1.0 / FIXED)
     doc_row = doc_ids[0]
     slot_range = jnp.arange(row_count)
     row_docs = (
@@ -307,8 +361,9 @@
     vec = picked_rows.astype(F32) + attn_out
     inv = lax.rsqrt(jnp.sum(vec * vec, axis=1, keepdims=True) + EPSILON)
     unit = vec * inv
-    all_fig = lax.all_gather(unit[:pair_count].astype(BF), "dp", axis=0, tiled=True)
-    all_cap = lax.all_gather(unit[pair_count:].astype(BF), "dp", axis=0, tiled=True)
+    all_emb = share(unit.astype(BF), dp_count)
+    all_fig = all_emb[:, :pair_count].reshape(-1, width)
+    all_cap = all_emb[:, pair_count:].reshape(-1, width)
     logit_mult = logit_scale[0]
     logits = logit_mult * mmt(all_fig, all_cap)
     row_lse = jnp.log(jnp.sum(jnp.exp(logits), axis=1))

time: 309 us -> 301 us (0.974)
  blocking collectives: 21.3 us -> 0 us
  Pallas kernels: 147 us -> 165 us
  starting transfers between devices: 10 us -> 4.63 us
  matrix products: 76.8 us -> 72.8 us
  local copies, waits for them, and re-layouts: 2.25 us -> 5.73 us
    all_gather x2 -> x0, blocking collectives: 21.3 us -> none  [the longest x1 11 us: body(): lax.all_gather(unit[pair_count:].astype(BF), 'dp', axis=0, tiled=True)]
    pallas_call x0 -> x1, Pallas kernels: none -> 16.3 us  [share(): pl.pallas_call(functools.partial(share_kernel, dp_count), out_shape=jax.S...]
    all_to_all x1 -> x0, starting transfers between devices: 5.17 us -> none  [body(): lax.all_to_all(send_ints, 'dp', split_axis=0, concat_axis=0, tiled=True)]
    dot_general x9, matrix products: 35.2 us -> 31.1 us  [mm(): return jnp.dot(a, b, preferred_element_type=F32)]
  transfers between devices with their start and end apart: 2 -> 1, of which waited for: 1 -> 1; matrix products, arithmetic and copies ran while one was open for 6% -> 0% of each run, Pallas kernels for 48% -> 0%
where the time goes in v2:
time: 301 us; the launch traced here: 300 us
  Pallas kernels  165 us (55%)
  matrix products  72.8 us (24%)
  waiting for transfers between devices  43 us (14%)
  other arithmetic  7.06 us (2%)
  local copies, waits for them, and re-layouts  5.73 us (2%)
  starting transfers between devices  4.63 us (2%)
    pallas_call x1, Pallas kernels, move(): pl.pallas_call(functools.partial(move_kernel, dp_count, fs_count, capacit...  149 us
    all_to_all x1, waiting for transfers between devices, body(): lax.all_to_all(row_ct.astype(BF), 'dp', split_axis=0, concat_axis=0, tile...  43 us
    dot_general x9, matrix products, mm(): return jnp.dot(a, b, preferred_element_type=F32)  31.1 us
    dot_general x5, matrix products, mmt(): lax.dot_general(a, b, (((1,), (1,)), ((), ())), preferred_element_type=F32)  19.4 us
    dot_general x4, matrix products, tmm(): lax.dot_general(a, b, (((0,), (0,)), ((), ())), preferred_element_type=F32)  18.1 us
    pallas_call x1, Pallas kernels, share(): pl.pallas_call(functools.partial(share_kernel, dp_count), out_shape=jax.S...  16.3 us
  transfers between devices with their start and end apart: 1, of which 1 were waited for; matrix products, arithmetic and copies ran while one was open for 0% of the time, Pallas kernels for 0%

profile of v2, /device:TPU:0, one launch (start us, length us, event | category | flops | bytes accessed | tf_op | source)
XLA Modules:
  0.0 300.3 jit_solution(4338401528626452095)
XLA Ops:
  0.6 0.0 copy-start
  0.7 0.9 add_select_fusion.2
  1.5 1.4 reduce-window.6
  2.9 0.1 slice.60
  3.0 0.1 copy.28
  3.2 0.2 reduce-window.9
  3.3 0.1 copy.29
  3.4 0.1 fusion.49
  3.5 0.7 fusion.64
  4.2 0.3 select_reduce_fusion.1
  4.5 0.1 sub.86
  4.6 0.7 multiply_convert_fusion.2
  5.3 0.1 pad.15.clone
  5.3 0.0 copy-done
  5.4 4.4 %convolution_convert_fusion.rows_ref = bf16[896,2048]{1,0:T(8,128)(2,1)} fusion(bf16[640,2048]{1,0:T(8,128)(2,1)S(1)} %copy-done, s32[640]{0:T(1024)S(1)} %get-tuple-element.30), kind=kOutput, calls=%fused_computation.8 | convolution fusion | flops 2351218688 | bytes 6294016 | tf_op jit(solution)/shard_map/dot_general | solution.py:19
  9.8 0.0 copy-done.9
  9.8 0.6 broadcast_in_dim.94.ints_ref
  10.4 149.2 %shard_map.104 = (bf16[896,2048]{1,0:T(8,128)(2,1)}, bf16[2048,1024]{1,0:T(8,128)(2,1)}, bf16[2048,2048]{1,0:T(8,128)(2,1)}, bf16[1024,2048]{1,0:T(8,128)(2,1)}, s32[8,8,128]{2,1,0:T(8,128)}) custom-call(bf16[896,2048]{1,0:T(8,128)(2,1)} %convolution_convert_fusion.rows_ref, bf16[3,512,1024]{2,1,0:T(8,128)(2,1)} %qkv_ref.1, bf16[1024,512]{1,0:T(8,128)(2,1)} %out_w_ref.1, ...), custom_call_target="tpu_custom_call" | custom-call | tf_op jit(solution)/shard_map/pallas_call | solution.py:219
  159.6 0.8 slice.47
  160.4 0.1 convert_multiply_fusion
  160.4 0.1 eq.174
  160.5 0.0 copy-done.15
  160.6 0.1 pad_add_fusion.1
  160.6 13.3 %convolution_convert_fusion.1 = bf16[896,2048]{1,0:T(8,128)(2,1)} fusion(bf16[896,2048]{1,0:T(8,128)(2,1)} %get-tuple-element.8, bf16[2048,2048]{1,0:T(8,128)(2,1)} %get-tuple-element.10), kind=kOutput, calls=%fused_computation.9 | convolution fusion | flops 7518027776 | bytes 15728640 | tf_op jit(solution)/shard_map/dot_general | solution.py:19
  173.9 0.7 convolution_convert_fusion.3
  174.6 0.5 select_reduce_fusion
  175.1 0.2 select_reduce_fusion.2
  175.3 0.0 copy-start.7
  175.3 0.0 copy-done.1
  175.4 0.8 convolution_convert_fusion.5
  176.2 0.0 copy-start.5
  176.2 0.1 broadcast_compare_fusion.1
  176.3 4.2 %fusion.20 = f32[16,32,896]{2,1,0:T(8,128)} fusion(bf16[896,2048]{1,0:T(8,128)(2,1)} %convolution_convert_fusion.1, pred[32,896]{1,0:T(8,128)(4,1)S(1)} %broadcast_compare_fusion.1, bf16[16,1024]{1,0:T(8,128)(2,1)S(1)} %get-tuple-element.27, bf16[32,1024]{1,0:T(8,128)(2,1)S(1)} %convolution_convert_fusion.5), kind=kOutput, calls=%fused_computation.37 | convolution fusion | flops 941426048 | bytes 3796992 | tf_op jit(solution)/shard_map/div | solution.py:356
  180.5 3.5 %multiply_reduce_fusion.1 = bf16[32,1024]{1,0:T(8,128)(2,1)S(1)} fusion(bf16[896,2048]{1,0:T(8,128)(2,1)} %convolution_convert_fusion.1, f32[16,1024]{1,0:T(8,128)S(1)} %get-tuple-element.28, f32[16,32,896]{2,1,0:T(8,128)} %fusion.20), kind=kOutput, calls=%fused_computation.19 | convolution fusion | flops 940998656 | bytes 3801088 | tf_op jit(solution)/shard_map/dot_general | solution.py:19
  184.0 0.9 multiply_reduce_fusion.4
  184.9 0.7 multiply_convert_fusion.1.emb_ref
  185.7 16.3 %shard_map.105 = bf16[8,32,2048]{2,1,0:T(8,128)(2,1)} custom-call(bf16[32,2048]{1,0:T(8,128)(2,1)} %multiply_convert_fusion.1.emb_ref), custom_call_target="tpu_custom_call" | custom-call | tf_op jit(solution)/shard_map/pallas_call | solution.py:278
  201.9 2.1 fusion.82
  204.7 0.1 mul.175
  204.8 1.4 select_reduce_fusion.3
  206.2 0.6 add_multiply_fusion
  206.8 0.1 fusion.41
  207.0 0.1 convert_subtract_fusion.2
  207.1 0.7 copy.31
  207.7 0.1 copy.32
  207.8 0.1 copy.33
  207.9 1.3 fusion.51
  209.2 0.9 fusion.57
  210.1 0.2 multiply_reduce_fusion.3
  210.3 3.7 %convolution_convert_fusion.4 = bf16[32,1024]{1,0:T(8,128)(2,1)S(1)} fusion(bf16[1024,2048]{1,0:T(8,128)(2,1)} %get-tuple-element.11, f32[32,2048]{1,0:T(8,128)S(1)} %get-tuple-element.37, f32[16,2048]{1,0:T(8,128)S(1)} %get-tuple-element.39, f32[16,2048]{1,0:T(8,128)S(1)} %get-tuple-element.40, f32[32]{0:T(128)S(1)} %multiply_reduce_fusion.3, ...), kind=kOutput, calls=%fused_computation.33 | convolution fusion | flops 134709248 | bytes 4784388 | tf_op jit(solution)/shard_map/dot_general | solution.py:23
  214.0 0.0 copy-done.19
  214.1 2.6 fusion.9
  216.6 5.3 %multiply_reduce_fusion = bf16[32,1024]{1,0:T(8,128)(2,1)S(1)} fusion(bf16[896,2048]{1,0:T(8,128)(2,1)} %convolution_convert_fusion.1, f32[16,1024]{1,0:T(8,128)S(1)} %copy-done.8, f32[16,32,896]{2,1,0:T(8,128)} %fusion.20, f32[16,32,896]{2,1,0:T(8,128)} %fusion.9), kind=kOutput, calls=%fused_computation.18 | convolution fusion | flops 942835072 | bytes 9306112 | tf_op jit(solution)/shard_map/dot_general | solution.py:19
  221.9 5.8 %bitcast_convert_fusion.1 = bf16[896,1024]{1,0:T(8,128)(2,1)} fusion(f32[16,32,896]{2,1,0:T(8,128)} %fusion.20, f32[16,32,896]{2,1,0:T(8,128)} %fusion.9, bf16[16,1024]{1,0:T(8,128)(2,1)S(1)} %get-tuple-element.27, bf16[32,1024]{1,0:T(8,128)(2,1)S(1)} %copy-done.6), kind=kOutput, calls=%fused_computation.7 | convolution fusion | flops 943261056 | bytes 5603328 | tf_op jit(solution)/shard_map/dot_general | solution.py:27
  227.8 2.8 bitcast_convert_fusion
  230.6 0.1 broadcast_compare_fusion
  230.7 1.4 subtract_convert_fusion
  232.1 0.1 copy-done.20
  232.2 10.3 %fusion.1 = f32[896,2048]{1,0:T(8,128)S(1)} fusion(bf16[2048,2048]{1,0:T(8,128)(2,1)} %get-tuple-element.10, bf16[896,1024]{1,0:T(8,128)(2,1)S(1)} %bitcast_convert_fusion, bf16[896,1024]{1,0:T(8,128)(2,1)S(1)} %copy-done.20), kind=kOutput, calls=%fused_computation.2 | convolution fusion | flops 7523532800 | bytes 19398656 | tf_op jit(solution)/shard_map/dot_general | solution.py:23
  242.5 3.1 %add_convert_fusion = bf16[896,2048]{1,0:T(8,128)(2,1)} fusion(f32[896,2048]{1,0:T(8,128)S(1)} %fusion.1, bf16[32,2048]{1,0:T(8,128)(2,1)S(1)} %get-tuple-element.17, bf16[32,2048]{1,0:T(8,128)(2,1)S(1)} %get-tuple-element.18, pred[32,896]{1,0:T(32,128)(4,1)S(1)} %broadcast_compare_fusion), kind=kOutput, calls=%fused_computation.1 | convolution fusion | flops 239132672 | bytes 11300864 | tf_op jit(solution)/shard_map/dot_general | solution.py:27
  245.6 4.6 %all-to-all-start = ((bf16[8,112,2048]{2,1,0:T(8,128)(2,1)}), bf16[8,112,2048]{2,1,0:T(8,128)(2,1)}, u32[]{:S(2)}, u32[]{:S(2)}) async-start(bf16[8,112,2048]{2,1,0:T(8,128)(2,1)} %bitcast.63), calls=%async_computation | async-start | bytes 7340032 | tf_op jit(solution)/shard_map/all_to_all | solution.py:401
  250.2 0.6 dynamic_slice.11
  250.8 43.0 %all-to-all-done = bf16[8,112,2048]{2,1,0:T(8,128)(2,1)} async-done(((bf16[8,112,2048]{2,1,0:T(8,128)(2,1)}), bf16[8,112,2048]{2,1,0:T(8,128)(2,1)}, u32[]{:S(2)}, u32[]{:S(2)}) %all-to-all-start) | async-done | bytes 3670048 | tf_op jit(solution)/shard_map/all_to_all | solution.py:401
  293.8 6.5 %convolution_convert_fusion.2 = bf16[640,2048]{1,0:T(8,128)(2,1)} fusion(bf16[896,2048]{1,0:T(8,128)(2,1)} %bitcast.14, s32[640]{0:T(1024)S(1)} %copy-done.10), kind=kOutput, calls=%fused_computation.10 | convolution fusion | flops 2350694400 | bytes 6294016 | tf_op jit(solution)/shard_map/dot_general | solution.py:27
  (43 shorter events, 0.2 us)
Async XLA Ops:
  0.6 4.7 %copy-start = (bf16[640,2048]{1,0:T(8,128)(2,1)S(1)}, bf16[640,2048]{1,0:T(8,128)(2,1)}, u32[]{:S(2)}) copy-start(bf16[640,2048]{1,0:T(8,128)(2,1)} %param.9) | copy-start | bytes 7864324
  4.2 5.6 %copy-start.9 = (s32[640]{0:T(1024)}, s32[640]{0:T(1024)S(1)}, u32[]{:S(2)}) copy-start(s32[640]{0:T(1024)S(1)} %get-tuple-element.30) | copy-start | bytes 7684
  10.4 150.1 %copy-start.15 = (s32[1,640]{1,0:T(1,128)S(1)}, s32[1,640]{1,0:T(1,128)}, u32[]{:S(2)}) copy-start(s32[1,640]{1,0:T(1,128)} %param.11) | copy-start | bytes 7684
  10.4 150.1 %copy-start.17 = (s32[16]{0:T(128)S(1)}, s32[16]{0:T(128)}, u32[]{:S(2)}) copy-start(s32[16]{0:T(128)} %param.15) | copy-start | bytes 196
  10.4 150.1 %copy-start.18 = (s32[16]{0:T(128)S(1)}, s32[16]{0:T(128)}, u32[]{:S(2)}) copy-start(s32[16]{0:T(128)} %param.14) | copy-start | bytes 196
  160.6 14.5 %copy-start.13 = (s32[32]{0:T(128)}, s32[32]{0:T(128)S(1)}, u32[]{:S(2)}) copy-start(s32[32]{0:T(128)S(1)} %pad_add_fusion.1) | copy-start | bytes 388
  160.6 13.3 %copy-start.4 = (bf16[896,2048]{1,0:T(8,128)(2,1)S(1)}, bf16[896,2048]{1,0:T(8,128)(2,1)}, u32[]{:S(2)}) copy-start(bf16[896,2048]{1,0:T(8,128)(2,1)} %get-tuple-element.8) | copy-start | bytes 11010052
  160.6 14.7 %copy-start.1 = (bf16[2048,1024]{1,0:T(8,128)(2,1)S(1)}, bf16[2048,1024]{1,0:T(8,128)(2,1)}, u32[]{:S(2)}) copy-start(bf16[2048,1024]{1,0:T(8,128)(2,1)} %get-tuple-element.9) | copy-start | bytes 12582916
  175.3 5.1 %copy-start.7 = (f32[16,1024]{1,0:T(8,128)}, f32[16,1024]{1,0:T(8,128)S(1)}, u32[]{:S(2)}) copy-start(f32[16,1024]{1,0:T(8,128)S(1)} %get-tuple-element.28) | copy-start | bytes 196612
  176.2 4.3 %copy-start.5 = (bf16[32,1024]{1,0:T(8,128)(2,1)}, bf16[32,1024]{1,0:T(8,128)(2,1)S(1)}, u32[]{:S(2)}) copy-start(bf16[32,1024]{1,0:T(8,128)(2,1)S(1)} %convolution_convert_fusion.5) | copy-start | bytes 196612
  180.5 3.5 %copy-start.3 = (bf16[1024,2048]{1,0:T(8,128)(2,1)S(1)}, bf16[1024,2048]{1,0:T(8,128)(2,1)}, u32[]{:S(2)}) copy-start(bf16[1024,2048]{1,0:T(8,128)(2,1)} %get-tuple-element.11) | copy-start | bytes 12582916
  184.9 21.3 %copy-start.11 = (f32[32]{0:T(128)}, f32[32]{0:T(128)S(1)}, u32[]{:S(2)}) copy-start(f32[32]{0:T(128)S(1)} %add_rsqrt_fusion) | copy-start | bytes 388
  207.7 2.4 copy-start.12
  210.3 3.7 %copy-start.19 = (bf16[896,2048]{1,0:T(8,128)(2,1)S(1)}, bf16[896,2048]{1,0:T(8,128)(2,1)}, u32[]{:S(2)}) copy-start(bf16[896,2048]{1,0:T(8,128)(2,1)} %convolution_convert_fusion.1) | copy-start | bytes 11010052
  214.0 2.6 copy-start.8
  216.6 5.3 %copy-start.6 = (bf16[32,1024]{1,0:T(8,128)(2,1)S(1)}, bf16[32,1024]{1,0:T(8,128)(2,1)}, u32[]{:S(2)}) copy-start(bf16[32,1024]{1,0:T(8,128)(2,1)} %copy-done.5) | copy-start | bytes 196612
  227.8 2.8 copy-start.14
  227.8 2.9 copy-start.2
  230.7 1.5 copy-start.20
  245.6 4.6 %copy-start.16 = (f32[128]{0:T(128)S(1)}, f32[128]{0:T(128)}, u32[]{:S(2)}) copy-start(f32[128]{0:T(128)} %get-tuple-element.33) | copy-start | bytes 1540
  245.6 48.3 %copy-start.10 = (s32[640]{0:T(1024)S(1)}, s32[640]{0:T(1024)}, u32[]{:S(2)}) copy-start(s32[640]{0:T(1024)} %copy-done.9) | copy-start | bytes 7684
  245.6 48.3 %all-to-all-start = ((bf16[8,112,2048]{2,1,0:T(8,128)(2,1)}), bf16[8,112,2048]{2,1,0:T(8,128)(2,1)}, u32[]{:S(2)}, u32[]{:S(2)}) async-start(bf16[8,112,2048]{2,1,0:T(8,128)(2,1)} %bitcast.63), calls=%async_computation | async-start | bytes 7340032 | tf_op jit(solution)/shard_map/all_to_all | solution.py:401

commit v3 on v2

--- a/solution.py
+++ b/solution.py
@@ -149,16 +149,21 @@
     )
     mine = regions(f, parity, chip)
     names = ("k", "v", "o", "q")
-    for i, name in enumerate(names):
+
+    def begin_z(i, name):
         for k in range(1, fs_count):
             begin(put(sources[name], mine[name], z_send.at[i, k], z_recv.at[i, k],
                       d, (f + k) % fs_count))
+
+    for i in range(3):
+        begin_z(i, names[i])
     for k in range(1, dp_count):
         to = (d + k) % dp_count
         begin(put(rows_ref.at[pl.ds(pl.multiple_of(to * capacity, 8), capacity), :],
                   got_ref.at[pl.ds(pl.multiple_of(d * capacity, 8), capacity), :],
                   page_send.at[k], page_recv.at[k], to, f))
         begin(put(ints_ref.at[to], got_ints_ref.at[d], ints_send.at[k], ints_recv.at[k], to, f))
+    begin_z(3, names[3])
     own = pl.ds(pl.multiple_of(d * capacity, 8), capacity)
     whole = at(f, 0, depth)
     locals_ = [

time: 301 us -> 301 us (level)
  no operation moved by 1% of the time
where the time goes in v3:
time: 301 us; the launch traced here: 300 us
  Pallas kernels  165 us (55%)
  matrix products  72.8 us (24%)
  waiting for transfers between devices  43 us (14%)
  other arithmetic  7.06 us (2%)
  local copies, waits for them, and re-layouts  5.73 us (2%)
  starting transfers between devices  4.63 us (2%)
    pallas_call x1, Pallas kernels, move(): pl.pallas_call(functools.partial(move_kernel, dp_count, fs_count, capacit...  149 us
    all_to_all x1, waiting for transfers between devices, body(): lax.all_to_all(row_ct.astype(BF), 'dp', split_axis=0, concat_axis=0, tile...  43 us
    dot_general x9, matrix products, mm(): return jnp.dot(a, b, preferred_element_type=F32)  31.1 us
    dot_general x5, matrix products, mmt(): lax.dot_general(a, b, (((1,), (1,)), ((), ())), preferred_element_type=F32)  19.4 us
    dot_general x4, matrix products, tmm(): lax.dot_general(a, b, (((0,), (0,)), ((), ())), preferred_element_type=F32)  18.1 us
    pallas_call x1, Pallas kernels, share(): pl.pallas_call(functools.partial(share_kernel, dp_count), out_shape=jax.S...  16.3 us
  transfers between devices with their start and end apart: 1, of which 1 were waited for; matrix products, arithmetic and copies ran while one was open for 0% of the time, Pallas kernels for 0%

profile of v3, /device:TPU:0, one launch (start us, length us, event | category | flops | bytes accessed | tf_op | source)
XLA Modules:
  0.0 300.3 jit_solution(1791065215724030816)
XLA Ops:
  0.6 0.0 copy-start
  0.7 0.9 add_select_fusion.2
  1.5 1.4 reduce-window.6
  2.9 0.1 slice.60
  3.0 0.1 copy.28
  3.2 0.2 reduce-window.9
  3.3 0.1 copy.29
  3.4 0.1 fusion.49
  3.5 0.7 fusion.64
  4.2 0.3 select_reduce_fusion.1
  4.5 0.1 sub.86
  4.6 0.7 multiply_convert_fusion.2
  5.3 0.1 pad.15.clone
  5.3 0.0 copy-done
  5.4 4.4 %convolution_convert_fusion.rows_ref = bf16[896,2048]{1,0:T(8,128)(2,1)} fusion(bf16[640,2048]{1,0:T(8,128)(2,1)S(1)} %copy-done, s32[640]{0:T(1024)S(1)} %get-tuple-element.30), kind=kOutput, calls=%fused_computation.8 | convolution fusion | flops 2351218688 | bytes 6294016 | tf_op jit(solution)/shard_map/dot_general | solution.py:19
  9.8 0.0 copy-done.9
  9.8 0.6 broadcast_in_dim.94.ints_ref
  10.4 149.2 %shard_map.104 = (bf16[896,2048]{1,0:T(8,128)(2,1)}, bf16[2048,1024]{1,0:T(8,128)(2,1)}, bf16[2048,2048]{1,0:T(8,128)(2,1)}, bf16[1024,2048]{1,0:T(8,128)(2,1)}, s32[8,8,128]{2,1,0:T(8,128)}) custom-call(bf16[896,2048]{1,0:T(8,128)(2,1)} %convolution_convert_fusion.rows_ref, bf16[3,512,1024]{2,1,0:T(8,128)(2,1)} %qkv_ref.1, bf16[1024,512]{1,0:T(8,128)(2,1)} %out_w_ref.1, ...), custom_call_target="tpu_custom_call" | custom-call | tf_op jit(solution)/shard_map/pallas_call | solution.py:224
  159.6 0.8 slice.47
  160.4 0.1 convert_multiply_fusion
  160.4 0.1 eq.174
  160.6 0.1 pad_add_fusion.1
  160.6 13.3 %convolution_convert_fusion.1 = bf16[896,2048]{1,0:T(8,128)(2,1)} fusion(bf16[896,2048]{1,0:T(8,128)(2,1)} %get-tuple-element.8, bf16[2048,2048]{1,0:T(8,128)(2,1)} %get-tuple-element.10), kind=kOutput, calls=%fused_computation.9 | convolution fusion | flops 7518027776 | bytes 15728640 | tf_op jit(solution)/shard_map/dot_general | solution.py:19
  173.9 0.0 copy-done.4
  173.9 0.7 convolution_convert_fusion.3
  174.6 0.5 select_reduce_fusion
  175.1 0.2 select_reduce_fusion.2
  175.3 0.0 copy-start.7
  175.3 0.0 copy-done.1
  175.4 0.8 convolution_convert_fusion.5
  176.2 0.0 copy-start.5
  176.2 0.1 broadcast_compare_fusion.1
  176.3 4.2 %fusion.20 = f32[16,32,896]{2,1,0:T(8,128)} fusion(bf16[896,2048]{1,0:T(8,128)(2,1)} %convolution_convert_fusion.1, pred[32,896]{1,0:T(8,128)(4,1)S(1)} %broadcast_compare_fusion.1, bf16[16,1024]{1,0:T(8,128)(2,1)S(1)} %get-tuple-element.27, bf16[32,1024]{1,0:T(8,128)(2,1)S(1)} %convolution_convert_fusion.5), kind=kOutput, calls=%fused_computation.37 | convolution fusion | flops 941426048 | bytes 3796992 | tf_op jit(solution)/shard_map/div | solution.py:361
  180.5 3.5 %multiply_reduce_fusion.1 = bf16[32,1024]{1,0:T(8,128)(2,1)S(1)} fusion(bf16[896,2048]{1,0:T(8,128)(2,1)} %convolution_convert_fusion.1, f32[16,1024]{1,0:T(8,128)S(1)} %get-tuple-element.28, f32[16,32,896]{2,1,0:T(8,128)} %fusion.20), kind=kOutput, calls=%fused_computation.19 | convolution fusion | flops 940998656 | bytes 3801088 | tf_op jit(solution)/shard_map/dot_general | solution.py:19
  184.0 0.9 multiply_reduce_fusion.4
  184.9 0.7 multiply_convert_fusion.1.emb_ref
  185.7 16.3 %shard_map.105 = bf16[8,32,2048]{2,1,0:T(8,128)(2,1)} custom-call(bf16[32,2048]{1,0:T(8,128)(2,1)} %multiply_convert_fusion.1.emb_ref), custom_call_target="tpu_custom_call" | custom-call | tf_op jit(solution)/shard_map/pallas_call | solution.py:283
  201.9 2.1 fusion.82
  204.7 0.1 mul.175
  204.8 1.4 select_reduce_fusion.3
  206.2 0.6 add_multiply_fusion
  206.8 0.1 fusion.41
  207.0 0.1 convert_subtract_fusion.2
  207.1 0.7 copy.31
  207.7 0.1 copy.32
  207.8 0.1 copy.33
  207.9 1.3 fusion.51
  209.2 0.9 fusion.57
  210.1 0.2 multiply_reduce_fusion.3
  210.3 3.7 %convolution_convert_fusion.4 = bf16[32,1024]{1,0:T(8,128)(2,1)S(1)} fusion(bf16[1024,2048]{1,0:T(8,128)(2,1)} %get-tuple-element.11, f32[32,2048]{1,0:T(8,128)S(1)} %get-tuple-element.37, f32[16,2048]{1,0:T(8,128)S(1)} %get-tuple-element.39, f32[16,2048]{1,0:T(8,128)S(1)} %get-tuple-element.40, f32[32]{0:T(128)S(1)} %multiply_reduce_fusion.3, ...), kind=kOutput, calls=%fused_computation.33 | convolution fusion | flops 134709248 | bytes 4784388 | tf_op jit(solution)/shard_map/dot_general | solution.py:23
  214.0 0.0 copy-done.19
  214.1 2.6 fusion.9
  216.6 5.3 %multiply_reduce_fusion = bf16[32,1024]{1,0:T(8,128)(2,1)S(1)} fusion(bf16[896,2048]{1,0:T(8,128)(2,1)} %convolution_convert_fusion.1, f32[16,1024]{1,0:T(8,128)S(1)} %copy-done.8, f32[16,32,896]{2,1,0:T(8,128)} %fusion.20, f32[16,32,896]{2,1,0:T(8,128)} %fusion.9), kind=kOutput, calls=%fused_computation.18 | convolution fusion | flops 942835072 | bytes 9306112 | tf_op jit(solution)/shard_map/dot_general | solution.py:19
  221.9 5.8 %bitcast_convert_fusion.1 = bf16[896,1024]{1,0:T(8,128)(2,1)} fusion(f32[16,32,896]{2,1,0:T(8,128)} %fusion.20, f32[16,32,896]{2,1,0:T(8,128)} %fusion.9, bf16[16,1024]{1,0:T(8,128)(2,1)S(1)} %get-tuple-element.27, bf16[32,1024]{1,0:T(8,128)(2,1)S(1)} %copy-done.6), kind=kOutput, calls=%fused_computation.7 | convolution fusion | flops 943261056 | bytes 5603328 | tf_op jit(solution)/shard_map/dot_general | solution.py:27
  227.8 2.8 bitcast_convert_fusion
  230.6 0.1 broadcast_compare_fusion
  230.7 1.4 subtract_convert_fusion
  232.1 0.1 copy-done.20
  232.2 10.3 %fusion.1 = f32[896,2048]{1,0:T(8,128)S(1)} fusion(bf16[2048,2048]{1,0:T(8,128)(2,1)} %get-tuple-element.10, bf16[896,1024]{1,0:T(8,128)(2,1)S(1)} %bitcast_convert_fusion, bf16[896,1024]{1,0:T(8,128)(2,1)S(1)} %copy-done.20), kind=kOutput, calls=%fused_computation.2 | convolution fusion | flops 7523532800 | bytes 19398656 | tf_op jit(solution)/shard_map/dot_general | solution.py:23
  242.5 3.1 %add_convert_fusion = bf16[896,2048]{1,0:T(8,128)(2,1)} fusion(f32[896,2048]{1,0:T(8,128)S(1)} %fusion.1, bf16[32,2048]{1,0:T(8,128)(2,1)S(1)} %get-tuple-element.17, bf16[32,2048]{1,0:T(8,128)(2,1)S(1)} %get-tuple-element.18, pred[32,896]{1,0:T(32,128)(4,1)S(1)} %broadcast_compare_fusion), kind=kOutput, calls=%fused_computation.1 | convolution fusion | flops 239132672 | bytes 11300864 | tf_op jit(solution)/shard_map/dot_general | solution.py:27
  245.6 4.6 %all-to-all-start = ((bf16[8,112,2048]{2,1,0:T(8,128)(2,1)}), bf16[8,112,2048]{2,1,0:T(8,128)(2,1)}, u32[]{:S(2)}, u32[]{:S(2)}) async-start(bf16[8,112,2048]{2,1,0:T(8,128)(2,1)} %bitcast.63), calls=%async_computation | async-start | bytes 7340032 | tf_op jit(solution)/shard_map/all_to_all | solution.py:406
  250.2 0.6 dynamic_slice.11
  250.8 43.0 %all-to-all-done = bf16[8,112,2048]{2,1,0:T(8,128)(2,1)} async-done(((bf16[8,112,2048]{2,1,0:T(8,128)(2,1)}), bf16[8,112,2048]{2,1,0:T(8,128)(2,1)}, u32[]{:S(2)}, u32[]{:S(2)}) %all-to-all-start) | async-done | bytes 3670048 | tf_op jit(solution)/shard_map/all_to_all | solution.py:406
  293.8 6.5 %convolution_convert_fusion.2 = bf16[640,2048]{1,0:T(8,128)(2,1)} fusion(bf16[896,2048]{1,0:T(8,128)(2,1)} %bitcast.14, s32[640]{0:T(1024)S(1)} %copy-done.10), kind=kOutput, calls=%fused_computation.10 | convolution fusion | flops 2350694400 | bytes 6294016 | tf_op jit(solution)/shard_map/dot_general | solution.py:27
  (43 shorter events, 0.2 us)
Async XLA Ops:
  0.6 4.7 %copy-start = (bf16[640,2048]{1,0:T(8,128)(2,1)S(1)}, bf16[640,2048]{1,0:T(8,128)(2,1)}, u32[]{:S(2)}) copy-start(bf16[640,2048]{1,0:T(8,128)(2,1)} %param.9) | copy-start | bytes 7864324
  4.2 5.6 %copy-start.9 = (s32[640]{0:T(1024)}, s32[640]{0:T(1024)S(1)}, u32[]{:S(2)}) copy-start(s32[640]{0:T(1024)S(1)} %get-tuple-element.30) | copy-start | bytes 7684
  10.4 150.1 %copy-start.15 = (s32[1,640]{1,0:T(1,128)S(1)}, s32[1,640]{1,0:T(1,128)}, u32[]{:S(2)}) copy-start(s32[1,640]{1,0:T(1,128)} %param.11) | copy-start | bytes 7684
  10.4 150.1 %copy-start.17 = (s32[16]{0:T(128)S(1)}, s32[16]{0:T(128)}, u32[]{:S(2)}) copy-start(s32[16]{0:T(128)} %param.15) | copy-start | bytes 196
  10.4 150.1 %copy-start.18 = (s32[16]{0:T(128)S(1)}, s32[16]{0:T(128)}, u32[]{:S(2)}) copy-start(s32[16]{0:T(128)} %param.14) | copy-start | bytes 196
  160.6 14.5 %copy-start.13 = (s32[32]{0:T(128)}, s32[32]{0:T(128)S(1)}, u32[]{:S(2)}) copy-start(s32[32]{0:T(128)S(1)} %pad_add_fusion.1) | copy-start | bytes 388
  160.6 13.3 %copy-start.4 = (bf16[896,2048]{1,0:T(8,128)(2,1)S(1)}, bf16[896,2048]{1,0:T(8,128)(2,1)}, u32[]{:S(2)}) copy-start(bf16[896,2048]{1,0:T(8,128)(2,1)} %get-tuple-element.8) | copy-start | bytes 11010052
  160.6 14.7 %copy-start.1 = (bf16[2048,1024]{1,0:T(8,128)(2,1)S(1)}, bf16[2048,1024]{1,0:T(8,128)(2,1)}, u32[]{:S(2)}) copy-start(bf16[2048,1024]{1,0:T(8,128)(2,1)} %get-tuple-element.9) | copy-start | bytes 12582916
  175.3 5.1 %copy-start.7 = (f32[16,1024]{1,0:T(8,128)}, f32[16,1024]{1,0:T(8,128)S(1)}, u32[]{:S(2)}) copy-start(f32[16,1024]{1,0:T(8,128)S(1)} %get-tuple-element.28) | copy-start | bytes 196612
  176.2 4.3 %copy-start.5 = (bf16[32,1024]{1,0:T(8,128)(2,1)}, bf16[32,1024]{1,0:T(8,128)(2,1)S(1)}, u32[]{:S(2)}) copy-start(bf16[32,1024]{1,0:T(8,128)(2,1)S(1)} %convolution_convert_fusion.5) | copy-start | bytes 196612
  180.5 3.5 %copy-start.3 = (bf16[1024,2048]{1,0:T(8,128)(2,1)S(1)}, bf16[1024,2048]{1,0:T(8,128)(2,1)}, u32[]{:S(2)}) copy-start(bf16[1024,2048]{1,0:T(8,128)(2,1)} %get-tuple-element.11) | copy-start | bytes 12582916
  184.9 21.3 %copy-start.11 = (f32[32]{0:T(128)}, f32[32]{0:T(128)S(1)}, u32[]{:S(2)}) copy-start(f32[32]{0:T(128)S(1)} %add_rsqrt_fusion) | copy-start | bytes 388
  207.7 2.4 copy-start.12
  210.3 3.7 %copy-start.19 = (bf16[896,2048]{1,0:T(8,128)(2,1)S(1)}, bf16[896,2048]{1,0:T(8,128)(2,1)}, u32[]{:S(2)}) copy-start(bf16[896,2048]{1,0:T(8,128)(2,1)} %convolution_convert_fusion.1) | copy-start | bytes 11010052
  214.0 2.6 copy-start.8
  216.6 5.3 %copy-start.6 = (bf16[32,1024]{1,0:T(8,128)(2,1)S(1)}, bf16[32,1024]{1,0:T(8,128)(2,1)}, u32[]{:S(2)}) copy-start(bf16[32,1024]{1,0:T(8,128)(2,1)} %copy-done.5) | copy-start | bytes 196612
  227.8 2.8 copy-start.14
  227.8 2.9 copy-start.2
  230.7 1.5 copy-start.20
  245.6 4.6 %copy-start.16 = (f32[128]{0:T(128)S(1)}, f32[128]{0:T(128)}, u32[]{:S(2)}) copy-start(f32[128]{0:T(128)} %get-tuple-element.33) | copy-start | bytes 1540
  245.6 48.3 %copy-start.10 = (s32[640]{0:T(1024)S(1)}, s32[640]{0:T(1024)}, u32[]{:S(2)}) copy-start(s32[640]{0:T(1024)} %copy-done.9) | copy-start | bytes 7684
  245.6 48.3 %all-to-all-start = ((bf16[8,112,2048]{2,1,0:T(8,128)(2,1)}), bf16[8,112,2048]{2,1,0:T(8,128)(2,1)}, u32[]{:S(2)}, u32[]{:S(2)}) async-start(bf16[8,112,2048]{2,1,0:T(8,128)(2,1)} %bitcast.63), calls=%async_computation | async-start | bytes 7340032 | tf_op jit(solution)/shard_map/all_to_all | solution.py:406
